TPU v7x, 128 devices: a whole 4x4x4 slice. The times are simulated.
128 devices in a mesh: row: 8 (over z, core), col: 8 (over x, y_lo), dp: 2 (over y_hi).
Axes of the slice: x: 4, y: 4 (y_hi: 2, y_lo: 2; y = y_hi * 2 + y_lo), z: 4, core: 2. Of those that a mesh axis runs over, the one named last changes fastest.
Arguments:
- inputs: bfloat16 [512, 12288], P(('col', 'dp'), 'row'), may hold values from -6 to 6
- out_grad: bfloat16 [512, 12288], P(('col', 'dp'), 'row'), may hold values from -6 to 6
- w_in: bfloat16 [12288, 24576], P('row', ('col', 'dp')), may hold values from -0.0546875 to 0.0546875
- bias_in: float32 [24576], P(('col', 'dp')), may hold values from -4 to 4
- w_out: bfloat16 [24576, 12288], P(('col', 'dp'), 'row'), may hold values from -0.0390625 to 0.0390625
Outputs:
- grad_inputs: bfloat16 [512, 12288], P(('col', 'dp'), 'row')
- grad_w_in: bfloat16 [12288, 24576], P('row', ('col', 'dp'))
- grad_bias: bfloat16 [24576], P(('col', 'dp'))
- grad_w_out: bfloat16 [24576, 12288], P(('col', 'dp'), 'row')
All inputs are finite; a program needn't handle non-finite values.
Results may differ from a plain program's by a relative error of at most 0.006.
Values may be sent and summed in bfloat16 or wider, within the bound.
No kernel may reach another device: no remote copies, remote signals or barrier semaphores. Data moves between devices by JAX's collectives and lax.ppermute only.
A program may use at most 128 MiB of HBM per device.

v0:
```python
import functools

import jax
import jax.numpy as jnp
from jax import lax
from jax.experimental import pallas as pl
from jax.experimental.pallas import tpu as pltpu
from jax.sharding import PartitionSpec as P

AXES = ("row", "col", "dp")
Z, CORES, X, Y = 4, 2, 4, 4
BF16, F32 = jnp.bfloat16, jnp.float32
STEPS = (0, 1, 3, 2)
TILE = 256
MIB = 1 << 20
LONG = 60 * 10**9


def place(z, core, x, y):
    return ((z * CORES + core) * 8 + x * 2 + y % 2) * 2 + y // 2


def pairs(source):
    every = [(z, c, x, y) for z in range(Z) for c in range(CORES) for x in range(X) for y in range(Y)]
    return [(place(*source(*at)), place(*at)) for at in every]


def along_first(step):
    return pairs(lambda z, c, x, y: (z, c, x, (y + step) % Y) if c else (z, c, (x + step) % X, y))


def along_second(step):
    return pairs(lambda z, c, x, y: (z, c, (x + step) % X, y) if c else (z, c, x, (y + step) % Y))


Z_ONE = pairs(lambda z, c, x, y: (z ^ (3 if c else 1), c, x, y))
Z_TWO = pairs(lambda z, c, x, y: (z ^ (1 if c else 3), c, x, y))


def along_z(step):
    return pairs(lambda z, c, x, y: ((z + step) % Z, c, x, y))


OTHER_CORE = pairs(lambda z, c, x, y: (z, 1 - c, x, y))


def send(value, perm):
    return lax.ppermute(value, AXES, perm)


def ring(value, along):
    return [send(value, along(STEPS[i])) for i in (3, 2, 1)][::-1]


def local(kernel, outs, args, limit=8, flops=0, follow=(), result=pltpu.VMEM):
    spec = pl.BlockSpec(memory_space=pltpu.VMEM)
    count = len(args)

    def run(*refs):
        kernel(*refs[:count], *refs[count + len(follow) :])

    args = [pltpu.with_memory_space_constraint(a, pltpu.VMEM) for a in args]
    moved = sum(a.size * a.dtype.itemsize for a in args)
    return pl.pallas_call(
        run,
        out_shape=[result(shape, dtype) for shape, dtype in outs],
        in_specs=[spec] * count + [pl.BlockSpec(memory_space=pltpu.HBM if f.size > 2**20 else pl.ANY) for f in follow],
        out_specs=[spec] * len(outs),
        compiler_params=pltpu.CompilerParams(vmem_limit_bytes=limit * MIB),
        cost_estimate=pl.CostEstimate(flops=flops, bytes_accessed=0, transcendentals=0),
    )(*args, *follow)


def at():
    row = lax.axis_index("row")
    z, core = row >> 1, row & 1
    return z, core, z ^ (1 + 2 * core), z ^ (3 - 2 * core)


def span(index, size):
    return pl.ds(pl.multiple_of(index * size, size), size)


def swapped_rows(ref, block, tokens):
    return jnp.concatenate([ref[span(a * 4 + block, tokens), :] for a in range(4)], axis=0)


def line_kernel(last, far, near, mine, ins, grads):
    tokens = mine.shape[1]
    for i, ref in enumerate((mine, near, far, last)):
        ins[i * tokens : (i + 1) * tokens, :] = ref[0]
        grads[i * tokens : (i + 1) * tokens, :] = ref[1]


def mark_kernel(out):
    out[...] = jnp.zeros_like(out)


def product_kernel(transposed, halves, d, c, b, a, weight, *outs):
    core = lax.axis_index("row") & 1
    rows = jnp.concatenate([a[...], b[...], c[...], d[...]], axis=0)
    for half, out in zip(halves, outs):
        tiles = out.shape[1] // TILE
        for n in range(tiles):
            part = span((core ^ half) * tiles + n, TILE)
            if transposed:
                value = lax.dot_general(
                    rows, weight[part, :], (((1,), (1,)), ((), ())), preferred_element_type=F32
                )
            else:
                value = jnp.dot(rows, weight[:, part], preferred_element_type=F32)
            out[:, n * TILE : (n + 1) * TILE] = value.astype(out.dtype)


def first_sum_kernel(keep, got, sent, mine, near):
    z, _, one, two = at()
    size = mine.shape[0]

    def block(index):
        return keep[span(index, size), :] + swapped_rows(got, index, size // 4).astype(F32)

    sent[0] = block(one).astype(BF16)
    sent[1] = block(z ^ 2).astype(BF16)
    near[...] = block(two)
    mine[...] = block(z)


def second_sum_kernel(mine, near, got, sent, out):
    sent[...] = (near[...] + got[1].astype(F32)).astype(BF16)
    out[...] = mine[...] + got[0].astype(F32)


def gelu_parts(value):
    scale = 0.7978845608028654
    inner = jnp.tanh(scale * (value + 0.044715 * value * value * value))
    slope = 0.5 * (1.0 + inner) + 0.5 * value * (1.0 - inner * inner) * (
        scale * (1.0 + 3.0 * 0.044715 * value * value)
    )
    return 0.5 * value * (1.0 + inner), slope


def activate_kernel(mine, got, bias, activated, slope):
    core = lax.axis_index("row") & 1
    value = mine[...] + got[...].astype(F32) + bias[:, span(core, mine.shape[1])]
    result, derivative = gelu_parts(value)
    activated[...] = result.astype(BF16)
    slope[...] = derivative


def pre_grad_kernel(mine, got, slope, out):
    out[...] = ((mine[...] + got[...].astype(F32)) * slope[...]).astype(BF16)


def pair_kernel(own, near, out):
    out[0] = own[...]
    out[1] = near[...]


def place_ring_kernel(two, three, one, own, out):
    z, size = at()[0], own.shape[0]
    for step, ref in enumerate((own, one, two, three)):
        out[span((z + step) & 3, size), :] = ref[...]


def copy_kernel(value, out):
    out[...] = value[...]


def place_kernel(own, near, far, out):
    z, _, one, two = at()
    size = own.shape[0]
    out[span(z, size), :] = own[...]
    out[span(two, size), :] = near[...]
    out[span(one, size), :] = far[0]
    out[span(z ^ 2, size), :] = far[1]


def orders_kernel(d, c, b, a, own, other):
    size = a.shape[0]
    tokens = size // 4
    for i, slab in enumerate((a, b, c, d)):
        own[i * size : (i + 1) * size, :] = slab[...]
        for k in range(4):
            other[k * size + i * tokens : k * size + (i + 1) * tokens, :] = slab[k * tokens : (k + 1) * tokens, :]


def share_own_kernel(mine, weight, out):
    core = lax.axis_index("row") & 1
    for n in range(out.shape[1] // TILE):
        tile = slice(n * TILE, (n + 1) * TILE)
        out[:, tile] = lax.dot_general(
            mine[...],
            weight[tile, span(core, mine.shape[1])],
            (((1,), (1,)), ((), ())),
            preferred_element_type=F32,
        )


def share_other_kernel(partial, other, weight, *outs):
    core = lax.axis_index("row") & 1
    size = outs[0].shape[0]
    rows = jnp.concatenate([swapped_rows(other, b, size // 4) for b in range(4)], axis=0)
    for n in range(partial.shape[1] // TILE):
        tile = slice(n * TILE, (n + 1) * TILE)
        value = partial[:, tile] + lax.dot_general(
            rows,
            weight[tile, span(1 - core, other.shape[1])],
            (((1,), (1,)), ((), ())),
            preferred_element_type=F32,
        )
        for b, out in enumerate(outs):
            out[:, tile] = value[b * size : (b + 1) * size].astype(out.dtype)


def line_sum_kernel(three, two, one, own, total, *sent):
    value = own[...] + one[...].astype(F32) + two[...].astype(F32) + three[...].astype(F32)
    tokens = total.shape[0]
    total[...] = value[:tokens]
    for i, out in enumerate(sent, 1):
        out[...] = value[i * tokens : (i + 1) * tokens].astype(BF16)


def last_sum_kernel(three, two, one, own, out):
    value = own[...] + one[...].astype(F32) + two[...].astype(F32) + three[...].astype(F32)
    out[...] = value.astype(BF16)


def fetch_kernel(source, follow, out, done):
    del follow
    copy = pltpu.make_async_copy(source, out, done)
    copy.start()
    copy.wait()


def fetch(weight, follow):
    return pl.pallas_call(
        fetch_kernel,
        out_shape=pltpu.VMEM(weight.shape, weight.dtype),
        in_specs=[pl.BlockSpec(memory_space=pltpu.HBM), pl.BlockSpec(memory_space=pl.ANY)],
        out_specs=pl.BlockSpec(memory_space=pltpu.VMEM),
        scratch_shapes=[pltpu.SemaphoreType.DMA],
        compiler_params=pltpu.CompilerParams(vmem_limit_bytes=MIB),
        cost_estimate=pl.CostEstimate(flops=0, bytes_accessed=0, transcendentals=0),
    )(weight, follow)


def grad_kernel(to_columns, left_own, left_other, right_own, right_other, *refs):
    out, total, tiles, sems = refs[-4:]
    core = lax.axis_index("row") & 1
    copies = []
    for i, (left, right) in enumerate(((left_own, right_own), (left_other, right_other))):
        half = core ^ i
        if to_columns:
            size = right.shape[1]
            total[:, span(half, size)] = jnp.sum(right[...].astype(F32), axis=0, keepdims=True)
        else:
            size = left.shape[1]
            total[...] = jnp.zeros_like(total)
        parts = tiles.shape[0] // 2
        width = tiles.shape[2]
        for n in range(parts):
            slot = i * parts + n
            part = slice(n * width, (n + 1) * width)
            tiles[slot] = lax.dot_general(
                left[...], right[:, part], (((0,), (0,)), ((), ())), preferred_element_type=F32
            ).astype(BF16)
            if to_columns:
                target = out.at[:, span(half * parts + n, width)]
            else:
                target = out.at[span(half, size), part]
            copies.append(pltpu.make_async_copy(tiles.at[slot], target, sems.at[slot]))
            copies[-1].start()
    for copy in copies:
        copy.wait()


def grad_of(left, right, to_columns, follow):
    every, rows = left[0].shape
    columns = right[0].shape[1]
    shape = (rows, 2 * columns) if to_columns else (2 * rows, columns)
    width = columns // (2 if to_columns else 3)
    parts = 2 * columns // width
    spec, whole = pl.BlockSpec(memory_space=pltpu.VMEM), pl.BlockSpec(memory_space=pltpu.HBM)
    args = [pltpu.with_memory_space_constraint(a, pltpu.VMEM) for a in [*left, *right]]
    return pl.pallas_call(
        functools.partial(grad_kernel, to_columns),
        out_shape=[jax.ShapeDtypeStruct(shape, BF16), pltpu.VMEM((1, shape[1]), F32)],
        in_specs=[spec] * 4 + [pl.BlockSpec(memory_space=pl.ANY)] * len(follow),
        out_specs=[whole, spec],
        scratch_shapes=[pltpu.VMEM((parts, rows, width), BF16), pltpu.SemaphoreType.DMA((parts,))],
        compiler_params=pltpu.CompilerParams(vmem_limit_bytes=20 * MIB),
        cost_estimate=pl.CostEstimate(flops=0, bytes_accessed=0, transcendentals=0),
    )(*args, *follow)


def both_orders(slabs):
    whole = ((4 * slabs[0].shape[0], slabs[0].shape[1]), BF16)
    return local(orders_kernel, [whole] * 2, slabs[::-1])


def body(inputs, out_grad, w_in, bias_in, w_out):
    tokens, features = inputs.shape
    hidden = w_in.shape[1]
    half, every, line = hidden // 2, 16 * tokens, 4 * tokens

    mine = jnp.stack([inputs, out_grad])
    steps = ring(mine, along_first)
    ins, grads = local(line_kernel, [((line, features), BF16)] * 2, steps[::-1] + [mine])
    ins = [ins] + ring(ins, along_second)
    grads = [grads] + ring(grads, along_second)

    w_in = fetch(w_in, ins[0])
    give, keep = ((every, half), BF16), ((every, half), F32)
    pre_give, pre_keep = local(
        functools.partial(product_kernel, False, (1, 0)), [give, keep], ins[::-1] + [w_in], 16, 0
    )
    quarter = (every // Z, half)

    def first_sum(given, kept, follow=()):
        sent, own, near = local(
            first_sum_kernel,
            [((2,) + quarter, BF16), (quarter, F32), (quarter, F32)],
            [kept, send(given, OTHER_CORE)],
            follow=follow,
        )
        return sent, [own, near, send(sent, Z_ONE)]

    (arrived,) = local(mark_kernel, [((8, 128), F32)], [], flops=LONG, follow=grads[1:])
    pre_sent, pre_sums = first_sum(pre_give, pre_keep, [arrived])
    (act_give,) = local(
        functools.partial(product_kernel, True, (1,)), [give], grads[::-1] + [w_out], 16, 0, [pre_sent]
    )
    (act_keep,) = local(
        functools.partial(product_kernel, True, (0,)), [keep], grads[::-1] + [w_out], 16, 0
    )
    act_sums = first_sum(act_give, act_keep)[1]
    in_orders = both_orders(ins)
    grad_orders = both_orders(grads)
    last = [(quarter, BF16), (quarter, F32)]
    pre_last, pre = local(second_sum_kernel, last, pre_sums, flops=LONG)
    activated, slope = local(
        activate_kernel, last, [pre, send(pre_last, Z_TWO), bias_in[None, :]], flops=LONG
    )
    act_last, act = local(
        second_sum_kernel, last, act_sums, follow=in_orders[:1] + grad_orders[:1]
    )
    (pre_grad,) = local(pre_grad_kernel, last[:1], [act, send(act_last, Z_TWO), slope])

    def paired(value, near, follow=()):
        return local(pair_kernel, [((2,) + quarter, BF16)], [value, near], follow=follow)[0]

    def placed(value, near, far, follow=()):
        return local(place_kernel, [((every, half), BF16)], [value, near, far], follow=follow)[0]

    def gathered(value, follow):
        return local(
            place_ring_kernel, [((every, half), BF16)], [send(value, along_z(d)) for d in (2, 3, 1)] + [value], follow=follow
        )[0]

    act_near = send(activated, Z_TWO)
    act_far = send(paired(activated, act_near), Z_ONE)
    pg_mine = gathered(pre_grad, [act_near])
    pg_other = send(pg_mine, OTHER_CORE)
    (partial,) = local(share_own_kernel, [((every, features), F32)], [pg_mine, w_in], 16, 0)
    share = local(
        share_other_kernel,
        [((line, features), F32)] + [((line, features), BF16)] * 3,
        [partial, pg_other, w_in],
        16,
        0,
    )
    got = [send(share[b], along_second(-STEPS[b])) for b in (3, 2, 1)]

    grad_w_in, grad_bias = grad_of(in_orders, (pg_mine, pg_other), True, [share[1]])
    grad_bias = grad_bias[0].astype(BF16)
    total, *sent = local(
        line_sum_kernel,
        [((tokens, features), F32)] + [((tokens, features), BF16)] * 3,
        got + [share[0]],
        follow=[grad_bias],
    )
    act_mine = placed(activated, act_near, act_far, [total])
    act_other = send(act_mine, OTHER_CORE)
    grad_w_out, done = grad_of((act_mine, act_other), grad_orders, False, [])
    (grad_inputs,) = local(
        last_sum_kernel,
        [((tokens, features), BF16)],
        [send(sent[a - 1], along_first(-STEPS[a])) for a in (3, 2, 1)] + [total],
        follow=[done],
        result=jax.ShapeDtypeStruct,
    )
    return (grad_inputs, grad_w_in, grad_bias, grad_w_out)


def solution(mesh):
    in_specs = (
        P(("col", "dp"), "row"),
        P(("col", "dp"), "row"),
        P("row", ("col", "dp")),
        P(("col", "dp")),
        P(("col", "dp"), "row"),
    )
    out_specs = (
        P(("col", "dp"), "row"),
        P("row", ("col", "dp")),
        P(("col", "dp")),
        P(("col", "dp"), "row"),
    )
    return jax.shard_map(body, mesh=mesh, in_specs=in_specs, out_specs=out_specs, check_vma=False)
```

profile of v0, /device:TPU:0, one launch (start us, length us, event | category | flops | bytes accessed | tf_op | source)
XLA Modules:
  0.0 96.9 jit_solution(17932165051783543830)
XLA Ops:
  1.6 3.2 %collective-permute-start = (bf16[2,32,1536]{2,1,0:T(8,128)(2,1)S(1)}, bf16[2,32,1536]{2,1,0:T(8,128)(2,1)S(1)}, u32[]{:S(2)}, u32[]{:S(2)}) collective-permute-start(bf16[2,32,1536]{2,1,0:T(8,128)(2,1)S(1)} %pad_maximum_fusion.refs_3_), channel_id=1, source_target_pairs={{8,0},{10,2},{9,1},{11,3},{12,4},{14,6},{13,5},{15,7},{0,8},{2,10}... | collective-permute-start | bytes 589832 | tf_op jit(solution)/shard_map/ppermute | solution.py:48
  5.4 2.6 %collective-permute-start.2 = (bf16[2,32,1536]{2,1,0:T(8,128)(2,1)S(1)}, bf16[2,32,1536]{2,1,0:T(8,128)(2,1)S(1)}, u32[]{:S(2)}, u32[]{:S(2)}) collective-permute-start(bf16[2,32,1536]{2,1,0:T(8,128)(2,1)S(1)} %pad_maximum_fusion.refs_3_), channel_id=1, source_target_pairs={{4,0},{6,2},{5,1},{7,3},{8,4},{10,6},{9,5},{11,7},{12,8},{14,10},{... | collective-permute-start | bytes 589832 | tf_op jit(solution)/shard_map/ppermute | solution.py:48
  8.8 2.8 %collective-permute-done.1.refs_1_ = bf16[2,32,1536]{2,1,0:T(8,128)(2,1)S(1)} collective-permute-done((bf16[2,32,1536]{2,1,0:T(8,128)(2,1)S(1)}, bf16[2,32,1536]{2,1,0:T(8,128)(2,1)S(1)}, u32[]{:S(2)}, u32[]{:S(2)}) %collective-permute-start.1) | collective-permute-done | bytes 196640 | tf_op jit(solution)/shard_map/ppermute | solution.py:48
  11.7 3.3 %collective-permute-start.6 = (bf16[128,1536]{1,0:T(8,128)(2,1)S(1)}, bf16[128,1536]{1,0:T(8,128)(2,1)S(1)}, u32[]{:S(2)}, u32[]{:S(2)}) collective-permute-start(bf16[128,1536]{1,0:T(8,128)(2,1)S(1)} %get-tuple-element.37.follow.refs_3_), channel_id=1, source_target_pairs={{1,0},{3,2},{0,1},{2,3},{5,4},{7,6},{4,5},{6,7},{9,8},{11,10},{8,9... | collective-permute-start | bytes 1179656 | tf_op jit(solution)/shard_map/ppermute | solution.py:48
  15.7 2.6 %collective-permute-start.8 = (bf16[128,1536]{1,0:T(8,128)(2,1)S(1)}, bf16[128,1536]{1,0:T(8,128)(2,1)S(1)}, u32[]{:S(2)}, u32[]{:S(2)}) collective-permute-start(bf16[128,1536]{1,0:T(8,128)(2,1)S(1)} %get-tuple-element.37.follow.refs_3_), channel_id=1, source_target_pairs={{2,0},{1,2},{3,1},{0,3},{6,4},{5,6},{7,5},{4,7},{10,8},{9,10},{11,... | collective-permute-start | bytes 1179656 | tf_op jit(solution)/shard_map/ppermute | solution.py:48
  19.1 2.1 %collective-permute-done.6.refs_0_ = bf16[128,1536]{1,0:T(8,128)(2,1)S(1)} collective-permute-done((bf16[128,1536]{1,0:T(8,128)(2,1)S(1)}, bf16[128,1536]{1,0:T(8,128)(2,1)S(1)}, u32[]{:S(2)}, u32[]{:S(2)}) %collective-permute-start.6) | collective-permute-done | bytes 393248 | tf_op jit(solution)/shard_map/ppermute | solution.py:48
  21.2 3.0 %collective-permute-start.5 = (bf16[128,1536]{1,0:T(8,128)(2,1)S(1)}, bf16[128,1536]{1,0:T(8,128)(2,1)S(1)}, u32[]{:S(2)}, u32[]{:S(2)}) collective-permute-start(bf16[128,1536]{1,0:T(8,128)(2,1)S(1)} %get-tuple-element.36.refs_3_), channel_id=1, source_target_pairs={{2,0},{1,2},{3,1},{0,3},{6,4},{5,6},{7,5},{4,7},{10,8},{9,10},{11,... | collective-permute-start | bytes 1179656 | tf_op jit(solution)/shard_map/ppermute | solution.py:48
  24.2 2.3 %copy-done.1 = bf16[1536,1536]{1,0:T(8,128)(2,1)S(1)} copy-done((bf16[1536,1536]{1,0:T(8,128)(2,1)S(1)}, bf16[1536,1536]{1,0:T(8,128)(2,1)}, u32[]{:S(2)}) %copy-start.1) | copy-done | bytes 4718616
  26.9 2.6 %shard_map.87 = (bf16[512,768]{1,0:T(8,128)(2,1)S(1)}, f32[512,768]{1,0:T(8,128)S(1)}) custom-call(bf16[128,1536]{1,0:T(8,128)(2,1)S(1)} %collective-permute-done.6.refs_0_, bf16[128,1536]{1,0:T(8,128)(2,1)S(1)} %collective-permute-done.7.refs_1_, bf16[128,1536]{1,0:T(8,128)(2,1)S(1)} %collective-permute-done.8.refs_2_, ...), custom_call_target="tpu_custom_call" | custom-call | tf_op jit(solution)/shard_map/pallas_call | solution.py:64
  29.7 4.0 %collective-permute-done.4.refs_1_ = bf16[128,1536]{1,0:T(8,128)(2,1)S(1)} collective-permute-done((bf16[128,1536]{1,0:T(8,128)(2,1)S(1)}, bf16[128,1536]{1,0:T(8,128)(2,1)S(1)}, u32[]{:S(2)}, u32[]{:S(2)}) %collective-permute-start.4) | collective-permute-done | bytes 393248 | tf_op jit(solution)/shard_map/ppermute | solution.py:48
  35.8 2.0 %collective-permute-start.13 = (bf16[2,128,768]{2,1,0:T(8,128)(2,1)S(1)}, bf16[2,128,768]{2,1,0:T(8,128)(2,1)S(1)}, u32[]{:S(2)}, u32[]{:S(2)}) collective-permute-start(bf16[2,128,768]{2,1,0:T(8,128)(2,1)S(1)} %get-tuple-element.40.refs_5_), channel_id=1, source_target_pairs={{32,0},{34,2},{33,1},{35,3},{36,4},{38,6},{37,5},{39,7},{40,8},{42... | collective-permute-start | bytes 1179656 | tf_op jit(solution)/shard_map/ppermute | solution.py:48
  40.2 3.4 %collective-permute-done.13.refs_2_ = bf16[2,128,768]{2,1,0:T(8,128)(2,1)S(1)} collective-permute-done((bf16[2,128,768]{2,1,0:T(8,128)(2,1)S(1)}, bf16[2,128,768]{2,1,0:T(8,128)(2,1)S(1)}, u32[]{:S(2)}, u32[]{:S(2)}) %collective-permute-start.13) | collective-permute-done | bytes 393248 | tf_op jit(solution)/shard_map/ppermute | solution.py:48
  43.7 4.1 %collective-permute-start.14 = (bf16[128,768]{1,0:T(8,128)(2,1)S(1)}, bf16[128,768]{1,0:T(8,128)(2,1)S(1)}, u32[]{:S(2)}, u32[]{:S(2)}) collective-permute-start(bf16[128,768]{1,0:T(8,128)(2,1)S(1)} %get-tuple-element.51), channel_id=1, source_target_pairs={{96,0},{98,2},{97,1},{99,3},{100,4},{102,6},{101,5},{103,7},{104,8... | collective-permute-start | bytes 589832 | tf_op jit(solution)/shard_map/ppermute | solution.py:48
  48.9 4.1 %collective-permute-start.12 = (bf16[128,768]{1,0:T(8,128)(2,1)S(1)}, bf16[128,768]{1,0:T(8,128)(2,1)S(1)}, u32[]{:S(2)}, u32[]{:S(2)}) collective-permute-start(bf16[128,768]{1,0:T(8,128)(2,1)S(1)} %get-tuple-element.47), channel_id=1, source_target_pairs={{96,0},{98,2},{97,1},{99,3},{100,4},{102,6},{101,5},{103,7},{104,8... | collective-permute-start | bytes 589832 | tf_op jit(solution)/shard_map/ppermute | solution.py:48
  56.7 2.0 %collective-permute-start.15 = (bf16[128,768]{1,0:T(8,128)(2,1)S(1)}, bf16[128,768]{1,0:T(8,128)(2,1)S(1)}, u32[]{:S(2)}, u32[]{:S(2)}) collective-permute-start(bf16[128,768]{1,0:T(8,128)(2,1)S(1)} %shard_map.97.refs_3_), channel_id=1, source_target_pairs={{64,0},{66,2},{65,1},{67,3},{68,4},{70,6},{69,5},{71,7},{72,8},{74... | collective-permute-start | bytes 589832 | tf_op jit(solution)/shard_map/ppermute | solution.py:48
  58.7 2.1 %collective-permute-start.16 = (bf16[128,768]{1,0:T(8,128)(2,1)S(1)}, bf16[128,768]{1,0:T(8,128)(2,1)S(1)}, u32[]{:S(2)}, u32[]{:S(2)}) collective-permute-start(bf16[128,768]{1,0:T(8,128)(2,1)S(1)} %shard_map.97.refs_3_), channel_id=1, source_target_pairs={{96,0},{98,2},{97,1},{99,3},{100,4},{102,6},{101,5},{103,7},{104,8... | collective-permute-start | bytes 589832 | tf_op jit(solution)/shard_map/ppermute | solution.py:48
  62.0 2.5 %collective-permute-done.18.refs_4_.refs_1_ = bf16[128,768]{1,0:T(8,128)(2,1)S(1)} collective-permute-done((bf16[128,768]{1,0:T(8,128)(2,1)S(1)}, bf16[128,768]{1,0:T(8,128)(2,1)S(1)}, u32[]{:S(2)}, u32[]{:S(2)}) %collective-permute-start.18) | collective-permute-done | bytes 196640 | tf_op jit(solution)/shard_map/ppermute | solution.py:48
  65.7 3.0 %collective-permute-done.16.refs_1_ = bf16[128,768]{1,0:T(8,128)(2,1)S(1)} collective-permute-done((bf16[128,768]{1,0:T(8,128)(2,1)S(1)}, bf16[128,768]{1,0:T(8,128)(2,1)S(1)}, u32[]{:S(2)}, u32[]{:S(2)}) %collective-permute-start.16) | collective-permute-done | bytes 196640 | tf_op jit(solution)/shard_map/ppermute | solution.py:48
  72.8 2.1 %collective-permute-start.20 = (bf16[128,1536]{1,0:T(8,128)(2,1)S(1)}, bf16[128,1536]{1,0:T(8,128)(2,1)S(1)}, u32[]{:S(2)}, u32[]{:S(2)}) collective-permute-start(bf16[128,1536]{1,0:T(8,128)(2,1)S(1)} %get-tuple-element.54), channel_id=1, source_target_pairs={{1,0},{3,2},{0,1},{2,3},{5,4},{7,6},{4,5},{6,7},{9,8},{11,10},{8,9... | collective-permute-start | bytes 1179656 | tf_op jit(solution)/shard_map/ppermute | solution.py:48
  74.9 2.0 %collective-permute-start.21 = (bf16[128,1536]{1,0:T(8,128)(2,1)S(1)}, bf16[128,1536]{1,0:T(8,128)(2,1)S(1)}, u32[]{:S(2)}, u32[]{:S(2)}) collective-permute-start(bf16[128,1536]{1,0:T(8,128)(2,1)S(1)} %get-tuple-element.55), channel_id=1, source_target_pairs={{2,0},{1,2},{3,1},{0,3},{6,4},{5,6},{7,5},{4,7},{10,8},{9,10},{11,... | collective-permute-start | bytes 1179656 | tf_op jit(solution)/shard_map/ppermute | solution.py:48
  77.1 4.7 %shard_map.101 = (bf16[1536,1536]{1,0:T(8,128)(2,1)}, f32[1,1536]{1,0:T(1,128)S(1)}) custom-call(bf16[512,1536]{1,0:T(8,128)(2,1)S(1)} %get-tuple-element.44.refs_3_.left_own, bf16[512,1536]{1,0:T(8,128)(2,1)S(1)} %get-tuple-element.58.left_other, bf16[512,768]{1,0:T(8,128)(2,1)S(1)} %shard_map.98.refs_0_.right_own, ...), custom_call_target="tpu_custom_call" | custom-call | tf_op jit(solution)/shard_map/pallas_call | solution.py:285
  82.2 4.2 %collective-permute-done.21.refs_1_ = bf16[128,1536]{1,0:T(8,128)(2,1)S(1)} collective-permute-done((bf16[128,1536]{1,0:T(8,128)(2,1)S(1)}, bf16[128,1536]{1,0:T(8,128)(2,1)S(1)}, u32[]{:S(2)}, u32[]{:S(2)}) %collective-permute-start.21) | collective-permute-done | bytes 393248 | tf_op jit(solution)/shard_map/ppermute | solution.py:48
  88.3 2.1 %collective-permute-start.24 = (bf16[32,1536]{1,0:T(8,128)(2,1)S(1)}, bf16[32,1536]{1,0:T(8,128)(2,1)S(1)}, u32[]{:S(2)}, u32[]{:S(2)}) collective-permute-start(bf16[32,1536]{1,0:T(8,128)(2,1)S(1)} %get-tuple-element.61), channel_id=1, source_target_pairs={{4,0},{6,2},{5,1},{7,3},{8,4},{10,6},{9,5},{11,7},{12,8},{14,10},{... | collective-permute-start | bytes 294920 | tf_op jit(solution)/shard_map/ppermute | solution.py:48
  90.9 3.6 %shard_map.105 = (bf16[1536,1536]{1,0:T(8,128)(2,1)}, f32[1,1536]{1,0:T(1,128)S(1)}) custom-call(bf16[512,768]{1,0:T(8,128)(2,1)S(1)} %shard_map.104.left_own, bf16[512,768]{1,0:T(8,128)(2,1)S(1)} %collective-permute-done.27.left_other, bf16[512,1536]{1,0:T(8,128)(2,1)S(1)} %get-tuple-element.45.refs_4_.right_own, ...), custom_call_target="tpu_custom_call" | custom-call | tf_op jit(solution)/shard_map/pallas_call | solution.py:285
  (76 shorter events, 25.3 us)
Async XLA Ops:
  1.6 7.3 %collective-permute-start = (bf16[2,32,1536]{2,1,0:T(8,128)(2,1)S(1)}, bf16[2,32,1536]{2,1,0:T(8,128)(2,1)S(1)}, u32[]{:S(2)}, u32[]{:S(2)}) collective-permute-start(bf16[2,32,1536]{2,1,0:T(8,128)(2,1)S(1)} %pad_maximum_fusion.refs_3_), channel_id=1, source_target_pairs={{8,0},{10,2},{9,1},{11,3},{12,4},{14,6},{13,5},{15,7},{0,8},{2,10}... | collective-permute-start | bytes 589832 | tf_op jit(solution)/shard_map/ppermute | solution.py:48
  4.8 6.9 %collective-permute-start.1 = (bf16[2,32,1536]{2,1,0:T(8,128)(2,1)S(1)}, bf16[2,32,1536]{2,1,0:T(8,128)(2,1)S(1)}, u32[]{:S(2)}, u32[]{:S(2)}) collective-permute-start(bf16[2,32,1536]{2,1,0:T(8,128)(2,1)S(1)} %pad_maximum_fusion.refs_3_), channel_id=1, source_target_pairs={{12,0},{14,2},{13,1},{15,3},{0,4},{2,6},{1,5},{3,7},{4,8},{6,10},{... | collective-permute-start | bytes 589832 | tf_op jit(solution)/shard_map/ppermute | solution.py:48
  5.4 6.3 %collective-permute-start.2 = (bf16[2,32,1536]{2,1,0:T(8,128)(2,1)S(1)}, bf16[2,32,1536]{2,1,0:T(8,128)(2,1)S(1)}, u32[]{:S(2)}, u32[]{:S(2)}) collective-permute-start(bf16[2,32,1536]{2,1,0:T(8,128)(2,1)S(1)} %pad_maximum_fusion.refs_3_), channel_id=1, source_target_pairs={{4,0},{6,2},{5,1},{7,3},{8,4},{10,6},{9,5},{11,7},{12,8},{14,10},{... | collective-permute-start | bytes 589832 | tf_op jit(solution)/shard_map/ppermute | solution.py:48
  11.7 9.5 %collective-permute-start.6 = (bf16[128,1536]{1,0:T(8,128)(2,1)S(1)}, bf16[128,1536]{1,0:T(8,128)(2,1)S(1)}, u32[]{:S(2)}, u32[]{:S(2)}) collective-permute-start(bf16[128,1536]{1,0:T(8,128)(2,1)S(1)} %get-tuple-element.37.follow.refs_3_), channel_id=1, source_target_pairs={{1,0},{3,2},{0,1},{2,3},{5,4},{7,6},{4,5},{6,7},{9,8},{11,10},{8,9... | collective-permute-start | bytes 1179656 | tf_op jit(solution)/shard_map/ppermute | solution.py:48
  15.0 11.9 %collective-permute-start.7 = (bf16[128,1536]{1,0:T(8,128)(2,1)S(1)}, bf16[128,1536]{1,0:T(8,128)(2,1)S(1)}, u32[]{:S(2)}, u32[]{:S(2)}) collective-permute-start(bf16[128,1536]{1,0:T(8,128)(2,1)S(1)} %get-tuple-element.37.follow.refs_3_), channel_id=1, source_target_pairs={{3,0},{0,2},{2,1},{1,3},{7,4},{4,6},{6,5},{5,7},{11,8},{8,10},{10,... | collective-permute-start | bytes 1179656 | tf_op jit(solution)/shard_map/ppermute | solution.py:48
  15.7 11.2 %collective-permute-start.8 = (bf16[128,1536]{1,0:T(8,128)(2,1)S(1)}, bf16[128,1536]{1,0:T(8,128)(2,1)S(1)}, u32[]{:S(2)}, u32[]{:S(2)}) collective-permute-start(bf16[128,1536]{1,0:T(8,128)(2,1)S(1)} %get-tuple-element.37.follow.refs_3_), channel_id=1, source_target_pairs={{2,0},{1,2},{3,1},{0,3},{6,4},{5,6},{7,5},{4,7},{10,8},{9,10},{11,... | collective-permute-start | bytes 1179656 | tf_op jit(solution)/shard_map/ppermute | solution.py:48
  18.2 11.4 %collective-permute-start.3 = (bf16[128,1536]{1,0:T(8,128)(2,1)S(1)}, bf16[128,1536]{1,0:T(8,128)(2,1)S(1)}, u32[]{:S(2)}, u32[]{:S(2)}) collective-permute-start(bf16[128,1536]{1,0:T(8,128)(2,1)S(1)} %get-tuple-element.36.refs_3_), channel_id=1, source_target_pairs={{1,0},{3,2},{0,1},{2,3},{5,4},{7,6},{4,5},{6,7},{9,8},{11,10},{8,9... | collective-permute-start | bytes 1179656 | tf_op jit(solution)/shard_map/ppermute | solution.py:48
  18.2 15.5 %collective-permute-start.4 = (bf16[128,1536]{1,0:T(8,128)(2,1)S(1)}, bf16[128,1536]{1,0:T(8,128)(2,1)S(1)}, u32[]{:S(2)}, u32[]{:S(2)}) collective-permute-start(bf16[128,1536]{1,0:T(8,128)(2,1)S(1)} %get-tuple-element.36.refs_3_), channel_id=1, source_target_pairs={{3,0},{0,2},{2,1},{1,3},{7,4},{4,6},{6,5},{5,7},{11,8},{8,10},{10,... | collective-permute-start | bytes 1179656 | tf_op jit(solution)/shard_map/ppermute | solution.py:48
  21.2 12.9 %collective-permute-start.5 = (bf16[128,1536]{1,0:T(8,128)(2,1)S(1)}, bf16[128,1536]{1,0:T(8,128)(2,1)S(1)}, u32[]{:S(2)}, u32[]{:S(2)}) collective-permute-start(bf16[128,1536]{1,0:T(8,128)(2,1)S(1)} %get-tuple-element.36.refs_3_), channel_id=1, source_target_pairs={{2,0},{1,2},{3,1},{0,3},{6,4},{5,6},{7,5},{4,7},{10,8},{9,10},{11,... | collective-permute-start | bytes 1179656 | tf_op jit(solution)/shard_map/ppermute | solution.py:48
  35.8 7.9 %collective-permute-start.13 = (bf16[2,128,768]{2,1,0:T(8,128)(2,1)S(1)}, bf16[2,128,768]{2,1,0:T(8,128)(2,1)S(1)}, u32[]{:S(2)}, u32[]{:S(2)}) collective-permute-start(bf16[2,128,768]{2,1,0:T(8,128)(2,1)S(1)} %get-tuple-element.40.refs_5_), channel_id=1, source_target_pairs={{32,0},{34,2},{33,1},{35,3},{36,4},{38,6},{37,5},{39,7},{40,8},{42... | collective-permute-start | bytes 1179656 | tf_op jit(solution)/shard_map/ppermute | solution.py:48
  39.4 9.4 %collective-permute-start.11 = (bf16[2,128,768]{2,1,0:T(8,128)(2,1)S(1)}, bf16[2,128,768]{2,1,0:T(8,128)(2,1)S(1)}, u32[]{:S(2)}, u32[]{:S(2)}) collective-permute-start(bf16[2,128,768]{2,1,0:T(8,128)(2,1)S(1)} %get-tuple-element.43), channel_id=1, source_target_pairs={{32,0},{34,2},{33,1},{35,3},{36,4},{38,6},{37,5},{39,7},{40,8},{42... | collective-permute-start | bytes 1179656 | tf_op jit(solution)/shard_map/ppermute | solution.py:48
  43.7 9.3 %collective-permute-start.14 = (bf16[128,768]{1,0:T(8,128)(2,1)S(1)}, bf16[128,768]{1,0:T(8,128)(2,1)S(1)}, u32[]{:S(2)}, u32[]{:S(2)}) collective-permute-start(bf16[128,768]{1,0:T(8,128)(2,1)S(1)} %get-tuple-element.51), channel_id=1, source_target_pairs={{96,0},{98,2},{97,1},{99,3},{100,4},{102,6},{101,5},{103,7},{104,8... | collective-permute-start | bytes 589832 | tf_op jit(solution)/shard_map/ppermute | solution.py:48
  48.9 7.8 %collective-permute-start.12 = (bf16[128,768]{1,0:T(8,128)(2,1)S(1)}, bf16[128,768]{1,0:T(8,128)(2,1)S(1)}, u32[]{:S(2)}, u32[]{:S(2)}) collective-permute-start(bf16[128,768]{1,0:T(8,128)(2,1)S(1)} %get-tuple-element.47), channel_id=1, source_target_pairs={{96,0},{98,2},{97,1},{99,3},{100,4},{102,6},{101,5},{103,7},{104,8... | collective-permute-start | bytes 589832 | tf_op jit(solution)/shard_map/ppermute | solution.py:48
  53.3 11.1 %collective-permute-start.18 = (bf16[128,768]{1,0:T(8,128)(2,1)S(1)}, bf16[128,768]{1,0:T(8,128)(2,1)S(1)}, u32[]{:S(2)}, u32[]{:S(2)}) collective-permute-start(bf16[128,768]{1,0:T(8,128)(2,1)S(1)} %get-tuple-element.53.refs_0_), channel_id=1, source_target_pairs={{96,0},{98,2},{97,1},{99,3},{100,4},{102,6},{101,5},{103,7},{104,8... | collective-permute-start | bytes 589832 | tf_op jit(solution)/shard_map/ppermute | solution.py:48
  56.7 9.1 %collective-permute-start.15 = (bf16[128,768]{1,0:T(8,128)(2,1)S(1)}, bf16[128,768]{1,0:T(8,128)(2,1)S(1)}, u32[]{:S(2)}, u32[]{:S(2)}) collective-permute-start(bf16[128,768]{1,0:T(8,128)(2,1)S(1)} %shard_map.97.refs_3_), channel_id=1, source_target_pairs={{64,0},{66,2},{65,1},{67,3},{68,4},{70,6},{69,5},{71,7},{72,8},{74... | collective-permute-start | bytes 589832 | tf_op jit(solution)/shard_map/ppermute | solution.py:48
  58.7 10.0 %collective-permute-start.16 = (bf16[128,768]{1,0:T(8,128)(2,1)S(1)}, bf16[128,768]{1,0:T(8,128)(2,1)S(1)}, u32[]{:S(2)}, u32[]{:S(2)}) collective-permute-start(bf16[128,768]{1,0:T(8,128)(2,1)S(1)} %shard_map.97.refs_3_), channel_id=1, source_target_pairs={{96,0},{98,2},{97,1},{99,3},{100,4},{102,6},{101,5},{103,7},{104,8... | collective-permute-start | bytes 589832 | tf_op jit(solution)/shard_map/ppermute | solution.py:48
  60.9 7.8 %collective-permute-start.17 = (bf16[128,768]{1,0:T(8,128)(2,1)S(1)}, bf16[128,768]{1,0:T(8,128)(2,1)S(1)}, u32[]{:S(2)}, u32[]{:S(2)}) collective-permute-start(bf16[128,768]{1,0:T(8,128)(2,1)S(1)} %shard_map.97.refs_3_), channel_id=1, source_target_pairs={{32,0},{34,2},{33,1},{35,3},{36,4},{38,6},{37,5},{39,7},{40,8},{42... | collective-permute-start | bytes 589832 | tf_op jit(solution)/shard_map/ppermute | solution.py:48
  72.8 9.4 %collective-permute-start.20 = (bf16[128,1536]{1,0:T(8,128)(2,1)S(1)}, bf16[128,1536]{1,0:T(8,128)(2,1)S(1)}, u32[]{:S(2)}, u32[]{:S(2)}) collective-permute-start(bf16[128,1536]{1,0:T(8,128)(2,1)S(1)} %get-tuple-element.54), channel_id=1, source_target_pairs={{1,0},{3,2},{0,1},{2,3},{5,4},{7,6},{4,5},{6,7},{9,8},{11,10},{8,9... | collective-permute-start | bytes 1179656 | tf_op jit(solution)/shard_map/ppermute | solution.py:48
  74.9 11.4 %collective-permute-start.21 = (bf16[128,1536]{1,0:T(8,128)(2,1)S(1)}, bf16[128,1536]{1,0:T(8,128)(2,1)S(1)}, u32[]{:S(2)}, u32[]{:S(2)}) collective-permute-start(bf16[128,1536]{1,0:T(8,128)(2,1)S(1)} %get-tuple-element.55), channel_id=1, source_target_pairs={{2,0},{1,2},{3,1},{0,3},{6,4},{5,6},{7,5},{4,7},{10,8},{9,10},{11,... | collective-permute-start | bytes 1179656 | tf_op jit(solution)/shard_map/ppermute | solution.py:48
  76.9 9.4 %collective-permute-start.22 = (bf16[128,1536]{1,0:T(8,128)(2,1)S(1)}, bf16[128,1536]{1,0:T(8,128)(2,1)S(1)}, u32[]{:S(2)}, u32[]{:S(2)}) collective-permute-start(bf16[128,1536]{1,0:T(8,128)(2,1)S(1)} %get-tuple-element.56.refs_0_), channel_id=1, source_target_pairs={{3,0},{0,2},{2,1},{1,3},{7,4},{4,6},{6,5},{5,7},{11,8},{8,10},{10,... | collective-permute-start | bytes 1179656 | tf_op jit(solution)/shard_map/ppermute | solution.py:48
  77.0 9.6 %collective-permute-start.26 = (bf16[2,128,768]{2,1,0:T(8,128)(2,1)S(1)}, bf16[2,128,768]{2,1,0:T(8,128)(2,1)S(1)}, u32[]{:S(2)}, u32[]{:S(2)}) collective-permute-start(bf16[2,128,768]{2,1,0:T(8,128)(2,1)S(1)} %shard_map.103), channel_id=1, source_target_pairs={{32,0},{34,2},{33,1},{35,3},{36,4},{38,6},{37,5},{39,7},{40,8},{42... | collective-permute-start | bytes 1179656 | tf_op jit(solution)/shard_map/ppermute | solution.py:48
  86.7 7.8 %collective-permute-start.23 = (bf16[32,1536]{1,0:T(8,128)(2,1)S(1)}, bf16[32,1536]{1,0:T(8,128)(2,1)S(1)}, u32[]{:S(2)}, u32[]{:S(2)}) collective-permute-start(bf16[32,1536]{1,0:T(8,128)(2,1)S(1)} %get-tuple-element.60), channel_id=1, source_target_pairs={{8,0},{10,2},{9,1},{11,3},{12,4},{14,6},{13,5},{15,7},{0,8},{2,10}... | collective-permute-start | bytes 294920 | tf_op jit(solution)/shard_map/ppermute | solution.py:48
  88.3 6.2 %collective-permute-start.24 = (bf16[32,1536]{1,0:T(8,128)(2,1)S(1)}, bf16[32,1536]{1,0:T(8,128)(2,1)S(1)}, u32[]{:S(2)}, u32[]{:S(2)}) collective-permute-start(bf16[32,1536]{1,0:T(8,128)(2,1)S(1)} %get-tuple-element.61), channel_id=1, source_target_pairs={{4,0},{6,2},{5,1},{7,3},{8,4},{10,6},{9,5},{11,7},{12,8},{14,10},{... | collective-permute-start | bytes 294920 | tf_op jit(solution)/shard_map/ppermute | solution.py:48
  90.4 5.8 %collective-permute-start.25 = (bf16[32,1536]{1,0:T(8,128)(2,1)S(1)}, bf16[32,1536]{1,0:T(8,128)(2,1)S(1)}, u32[]{:S(2)}, u32[]{:S(2)}) collective-permute-start(bf16[32,1536]{1,0:T(8,128)(2,1)S(1)} %get-tuple-element.62), channel_id=1, source_target_pairs={{12,0},{14,2},{13,1},{15,3},{0,4},{2,6},{1,5},{3,7},{4,8},{6,10},{... | collective-permute-start | bytes 294920 | tf_op jit(solution)/shard_map/ppermute | solution.py:48
  (12 other events, 80.9 us)
where the time goes:
time: 97.5 us; the launch traced here: 96.9 us
  starting transfers between devices  44 us (45%)
  waiting for transfers between devices  29.4 us (30%)
  Pallas kernels  19.2 us (20%)
  local copies, waits for them, and re-layouts  2.38 us (2%)
  other arithmetic  0.99 us (1%)
    ppermute x28, starting transfers between devices, send(): return lax.ppermute(value, AXES, perm)  44 us
    ppermute x28, waiting for transfers between devices, send(): return lax.ppermute(value, AXES, perm)  29.4 us
    pallas_call x20, Pallas kernels, local(): pl.pallas_call(run, out_shape=[result(shape, dtype) for shape, dtype in o...  10.6 us
    pallas_call x2, Pallas kernels, grad_of(): pl.pallas_call(functools.partial(grad_kernel, to_columns), out_shape=[jax...  8.32 us
    unnamed x16, local copies, waits for them, and re-layouts  2.37 us
  transfers between devices with their start and end apart: 28, of which 15 were waited for; matrix products, arithmetic and copies ran while one was open for 0% of the time, Pallas kernels for 16%

commit v1 on v0

--- a/solution.py
+++ b/solution.py
@@ -170,8 +170,8 @@
     z, _, one, two = at()
     size = own.shape[0]
     out[span(z, size), :] = own[...]
-    out[span(two, size), :] = near[...]
-    out[span(one, size), :] = far[0]
+    out[span(one, size), :] = near[...]
+    out[span(two, size), :] = far[0]
     out[span(z ^ 2, size), :] = far[1]
 
 
@@ -357,8 +357,8 @@
             place_ring_kernel, [((every, half), BF16)], [send(value, along_z(d)) for d in (2, 3, 1)] + [value], follow=follow
         )[0]
 
-    act_near = send(activated, Z_TWO)
-    act_far = send(paired(activated, act_near), Z_ONE)
+    act_near = send(activated, Z_ONE)
+    act_far = send(paired(activated, act_near), Z_TWO)
     pg_mine = gathered(pre_grad, [act_near])
     pg_other = send(pg_mine, OTHER_CORE)
     (partial,) = local(share_own_kernel, [((every, features), F32)], [pg_mine, w_in], 16, 0)

time: 97.5 us -> 97.3 us (level)
  waiting for transfers between devices: 29.4 us -> 27.9 us
  starting transfers between devices: 44 us -> 45.3 us
    ppermute x28, waiting for transfers between devices: 29.4 us -> 27.9 us  [send(): return lax.ppermute(value, AXES, perm)]
    ppermute x28, starting transfers between devices: 44 us -> 45.3 us  [send(): return lax.ppermute(value, AXES, perm)]
  transfers between devices with their start and end apart: 28 -> 28, of which waited for: 15 -> 13; matrix products, arithmetic and copies ran while one was open for 0% -> 0% of each run, Pallas kernels for 16% -> 16%
where the time goes in v1:
time: 97.3 us; the launch traced here: 96.7 us
  starting transfers between devices  45.3 us (47%)
  waiting for transfers between devices  27.9 us (29%)
  Pallas kernels  19.2 us (20%)
  local copies, waits for them, and re-layouts  2.38 us (2%)
  other arithmetic  0.99 us (1%)
    ppermute x28, starting transfers between devices, send(): return lax.ppermute(value, AXES, perm)  45.3 us
    ppermute x28, waiting for transfers between devices, send(): return lax.ppermute(value, AXES, perm)  27.9 us
    pallas_call x20, Pallas kernels, local(): pl.pallas_call(run, out_shape=[result(shape, dtype) for shape, dtype in o...  10.6 us
    pallas_call x2, Pallas kernels, grad_of(): pl.pallas_call(functools.partial(grad_kernel, to_columns), out_shape=[jax...  8.32 us
    unnamed x16, local copies, waits for them, and re-layouts  2.37 us
  transfers between devices with their start and end apart: 28, of which 13 were waited for; matrix products, arithmetic and copies ran while one was open for 0% of the time, Pallas kernels for 16%

profile of v1, /device:TPU:0, one launch (start us, length us, event | category | flops | bytes accessed | tf_op | source)
XLA Modules:
  0.0 96.7 jit_solution(6835439621474008066)
XLA Ops:
  1.6 3.2 %collective-permute-start = (bf16[2,32,1536]{2,1,0:T(8,128)(2,1)S(1)}, bf16[2,32,1536]{2,1,0:T(8,128)(2,1)S(1)}, u32[]{:S(2)}, u32[]{:S(2)}) collective-permute-start(bf16[2,32,1536]{2,1,0:T(8,128)(2,1)S(1)} %pad_maximum_fusion.refs_3_), channel_id=1, source_target_pairs={{8,0},{10,2},{9,1},{11,3},{12,4},{14,6},{13,5},{15,7},{0,8},{2,10}... | collective-permute-start | bytes 589832 | tf_op jit(solution)/shard_map/ppermute | solution.py:48
  5.4 2.6 %collective-permute-start.2 = (bf16[2,32,1536]{2,1,0:T(8,128)(2,1)S(1)}, bf16[2,32,1536]{2,1,0:T(8,128)(2,1)S(1)}, u32[]{:S(2)}, u32[]{:S(2)}) collective-permute-start(bf16[2,32,1536]{2,1,0:T(8,128)(2,1)S(1)} %pad_maximum_fusion.refs_3_), channel_id=1, source_target_pairs={{4,0},{6,2},{5,1},{7,3},{8,4},{10,6},{9,5},{11,7},{12,8},{14,10},{... | collective-permute-start | bytes 589832 | tf_op jit(solution)/shard_map/ppermute | solution.py:48
  8.8 2.8 %collective-permute-done.1.refs_1_ = bf16[2,32,1536]{2,1,0:T(8,128)(2,1)S(1)} collective-permute-done((bf16[2,32,1536]{2,1,0:T(8,128)(2,1)S(1)}, bf16[2,32,1536]{2,1,0:T(8,128)(2,1)S(1)}, u32[]{:S(2)}, u32[]{:S(2)}) %collective-permute-start.1) | collective-permute-done | bytes 196640 | tf_op jit(solution)/shard_map/ppermute | solution.py:48
  11.7 3.3 %collective-permute-start.6 = (bf16[128,1536]{1,0:T(8,128)(2,1)S(1)}, bf16[128,1536]{1,0:T(8,128)(2,1)S(1)}, u32[]{:S(2)}, u32[]{:S(2)}) collective-permute-start(bf16[128,1536]{1,0:T(8,128)(2,1)S(1)} %get-tuple-element.37.follow.refs_3_), channel_id=1, source_target_pairs={{1,0},{3,2},{0,1},{2,3},{5,4},{7,6},{4,5},{6,7},{9,8},{11,10},{8,9... | collective-permute-start | bytes 1179656 | tf_op jit(solution)/shard_map/ppermute | solution.py:48
  15.7 2.6 %collective-permute-start.8 = (bf16[128,1536]{1,0:T(8,128)(2,1)S(1)}, bf16[128,1536]{1,0:T(8,128)(2,1)S(1)}, u32[]{:S(2)}, u32[]{:S(2)}) collective-permute-start(bf16[128,1536]{1,0:T(8,128)(2,1)S(1)} %get-tuple-element.37.follow.refs_3_), channel_id=1, source_target_pairs={{2,0},{1,2},{3,1},{0,3},{6,4},{5,6},{7,5},{4,7},{10,8},{9,10},{11,... | collective-permute-start | bytes 1179656 | tf_op jit(solution)/shard_map/ppermute | solution.py:48
  19.1 2.1 %collective-permute-done.6.refs_0_ = bf16[128,1536]{1,0:T(8,128)(2,1)S(1)} collective-permute-done((bf16[128,1536]{1,0:T(8,128)(2,1)S(1)}, bf16[128,1536]{1,0:T(8,128)(2,1)S(1)}, u32[]{:S(2)}, u32[]{:S(2)}) %collective-permute-start.6) | collective-permute-done | bytes 393248 | tf_op jit(solution)/shard_map/ppermute | solution.py:48
  21.2 3.0 %collective-permute-start.5 = (bf16[128,1536]{1,0:T(8,128)(2,1)S(1)}, bf16[128,1536]{1,0:T(8,128)(2,1)S(1)}, u32[]{:S(2)}, u32[]{:S(2)}) collective-permute-start(bf16[128,1536]{1,0:T(8,128)(2,1)S(1)} %get-tuple-element.36.refs_3_), channel_id=1, source_target_pairs={{2,0},{1,2},{3,1},{0,3},{6,4},{5,6},{7,5},{4,7},{10,8},{9,10},{11,... | collective-permute-start | bytes 1179656 | tf_op jit(solution)/shard_map/ppermute | solution.py:48
  24.2 2.3 %copy-done.1 = bf16[1536,1536]{1,0:T(8,128)(2,1)S(1)} copy-done((bf16[1536,1536]{1,0:T(8,128)(2,1)S(1)}, bf16[1536,1536]{1,0:T(8,128)(2,1)}, u32[]{:S(2)}) %copy-start.1) | copy-done | bytes 4718616
  26.9 2.6 %shard_map.87 = (bf16[512,768]{1,0:T(8,128)(2,1)S(1)}, f32[512,768]{1,0:T(8,128)S(1)}) custom-call(bf16[128,1536]{1,0:T(8,128)(2,1)S(1)} %collective-permute-done.6.refs_0_, bf16[128,1536]{1,0:T(8,128)(2,1)S(1)} %collective-permute-done.7.refs_1_, bf16[128,1536]{1,0:T(8,128)(2,1)S(1)} %collective-permute-done.8.refs_2_, ...), custom_call_target="tpu_custom_call" | custom-call | tf_op jit(solution)/shard_map/pallas_call | solution.py:64
  29.7 4.0 %collective-permute-done.4.refs_1_ = bf16[128,1536]{1,0:T(8,128)(2,1)S(1)} collective-permute-done((bf16[128,1536]{1,0:T(8,128)(2,1)S(1)}, bf16[128,1536]{1,0:T(8,128)(2,1)S(1)}, u32[]{:S(2)}, u32[]{:S(2)}) %collective-permute-start.4) | collective-permute-done | bytes 393248 | tf_op jit(solution)/shard_map/ppermute | solution.py:48
  35.8 2.0 %collective-permute-start.13 = (bf16[2,128,768]{2,1,0:T(8,128)(2,1)S(1)}, bf16[2,128,768]{2,1,0:T(8,128)(2,1)S(1)}, u32[]{:S(2)}, u32[]{:S(2)}) collective-permute-start(bf16[2,128,768]{2,1,0:T(8,128)(2,1)S(1)} %get-tuple-element.40.refs_5_), channel_id=1, source_target_pairs={{32,0},{34,2},{33,1},{35,3},{36,4},{38,6},{37,5},{39,7},{40,8},{42... | collective-permute-start | bytes 1179656 | tf_op jit(solution)/shard_map/ppermute | solution.py:48
  40.2 3.4 %collective-permute-done.13.refs_2_ = bf16[2,128,768]{2,1,0:T(8,128)(2,1)S(1)} collective-permute-done((bf16[2,128,768]{2,1,0:T(8,128)(2,1)S(1)}, bf16[2,128,768]{2,1,0:T(8,128)(2,1)S(1)}, u32[]{:S(2)}, u32[]{:S(2)}) %collective-permute-start.13) | collective-permute-done | bytes 393248 | tf_op jit(solution)/shard_map/ppermute | solution.py:48
  43.7 4.1 %collective-permute-start.14 = (bf16[128,768]{1,0:T(8,128)(2,1)S(1)}, bf16[128,768]{1,0:T(8,128)(2,1)S(1)}, u32[]{:S(2)}, u32[]{:S(2)}) collective-permute-start(bf16[128,768]{1,0:T(8,128)(2,1)S(1)} %get-tuple-element.51), channel_id=1, source_target_pairs={{96,0},{98,2},{97,1},{99,3},{100,4},{102,6},{101,5},{103,7},{104,8... | collective-permute-start | bytes 589832 | tf_op jit(solution)/shard_map/ppermute | solution.py:48
  48.9 4.1 %collective-permute-start.12 = (bf16[128,768]{1,0:T(8,128)(2,1)S(1)}, bf16[128,768]{1,0:T(8,128)(2,1)S(1)}, u32[]{:S(2)}, u32[]{:S(2)}) collective-permute-start(bf16[128,768]{1,0:T(8,128)(2,1)S(1)} %get-tuple-element.47), channel_id=1, source_target_pairs={{96,0},{98,2},{97,1},{99,3},{100,4},{102,6},{101,5},{103,7},{104,8... | collective-permute-start | bytes 589832 | tf_op jit(solution)/shard_map/ppermute | solution.py:48
  53.4 4.5 %collective-permute-done.12.refs_1_ = bf16[128,768]{1,0:T(8,128)(2,1)S(1)} collective-permute-done((bf16[128,768]{1,0:T(8,128)(2,1)S(1)}, bf16[128,768]{1,0:T(8,128)(2,1)S(1)}, u32[]{:S(2)}, u32[]{:S(2)}) %collective-permute-start.12) | collective-permute-done | bytes 196640 | tf_op jit(solution)/shard_map/ppermute | solution.py:48
  57.9 2.6 %collective-permute-start.15 = (bf16[128,768]{1,0:T(8,128)(2,1)S(1)}, bf16[128,768]{1,0:T(8,128)(2,1)S(1)}, u32[]{:S(2)}, u32[]{:S(2)}) collective-permute-start(bf16[128,768]{1,0:T(8,128)(2,1)S(1)} %shard_map.97.refs_3_), channel_id=1, source_target_pairs={{64,0},{66,2},{65,1},{67,3},{68,4},{70,6},{69,5},{71,7},{72,8},{74... | collective-permute-start | bytes 589832 | tf_op jit(solution)/shard_map/ppermute | solution.py:48
  63.8 2.8 %collective-permute-done.15.refs_0_ = bf16[128,768]{1,0:T(8,128)(2,1)S(1)} collective-permute-done((bf16[128,768]{1,0:T(8,128)(2,1)S(1)}, bf16[128,768]{1,0:T(8,128)(2,1)S(1)}, u32[]{:S(2)}, u32[]{:S(2)}) %collective-permute-start.15) | collective-permute-done | bytes 196640 | tf_op jit(solution)/shard_map/ppermute | solution.py:48
  72.5 2.1 %collective-permute-start.20 = (bf16[128,1536]{1,0:T(8,128)(2,1)S(1)}, bf16[128,1536]{1,0:T(8,128)(2,1)S(1)}, u32[]{:S(2)}, u32[]{:S(2)}) collective-permute-start(bf16[128,1536]{1,0:T(8,128)(2,1)S(1)} %get-tuple-element.54), channel_id=1, source_target_pairs={{1,0},{3,2},{0,1},{2,3},{5,4},{7,6},{4,5},{6,7},{9,8},{11,10},{8,9... | collective-permute-start | bytes 1179656 | tf_op jit(solution)/shard_map/ppermute | solution.py:48
  74.7 2.1 %collective-permute-start.21 = (bf16[128,1536]{1,0:T(8,128)(2,1)S(1)}, bf16[128,1536]{1,0:T(8,128)(2,1)S(1)}, u32[]{:S(2)}, u32[]{:S(2)}) collective-permute-start(bf16[128,1536]{1,0:T(8,128)(2,1)S(1)} %get-tuple-element.55), channel_id=1, source_target_pairs={{2,0},{1,2},{3,1},{0,3},{6,4},{5,6},{7,5},{4,7},{10,8},{9,10},{11,... | collective-permute-start | bytes 1179656 | tf_op jit(solution)/shard_map/ppermute | solution.py:48
  76.8 2.5 %collective-permute-start.26 = (bf16[2,128,768]{2,1,0:T(8,128)(2,1)S(1)}, bf16[2,128,768]{2,1,0:T(8,128)(2,1)S(1)}, u32[]{:S(2)}, u32[]{:S(2)}) collective-permute-start(bf16[2,128,768]{2,1,0:T(8,128)(2,1)S(1)} %shard_map.103), channel_id=1, source_target_pairs={{96,0},{98,2},{97,1},{99,3},{100,4},{102,6},{101,5},{103,7},{104,8... | collective-permute-start | bytes 1179656 | tf_op jit(solution)/shard_map/ppermute | solution.py:48
  79.3 4.7 %shard_map.101 = (bf16[1536,1536]{1,0:T(8,128)(2,1)}, f32[1,1536]{1,0:T(1,128)S(1)}) custom-call(bf16[512,1536]{1,0:T(8,128)(2,1)S(1)} %get-tuple-element.44.refs_3_.left_own, bf16[512,1536]{1,0:T(8,128)(2,1)S(1)} %get-tuple-element.58.left_other, bf16[512,768]{1,0:T(8,128)(2,1)S(1)} %shard_map.98.refs_0_.right_own, ...), custom_call_target="tpu_custom_call" | custom-call | tf_op jit(solution)/shard_map/pallas_call | solution.py:285
  84.1 2.0 %collective-permute-done.21.refs_1_ = bf16[128,1536]{1,0:T(8,128)(2,1)S(1)} collective-permute-done((bf16[128,1536]{1,0:T(8,128)(2,1)S(1)}, bf16[128,1536]{1,0:T(8,128)(2,1)S(1)}, u32[]{:S(2)}, u32[]{:S(2)}) %collective-permute-start.21) | collective-permute-done | bytes 393248 | tf_op jit(solution)/shard_map/ppermute | solution.py:48
  88.1 2.1 %collective-permute-start.24 = (bf16[32,1536]{1,0:T(8,128)(2,1)S(1)}, bf16[32,1536]{1,0:T(8,128)(2,1)S(1)}, u32[]{:S(2)}, u32[]{:S(2)}) collective-permute-start(bf16[32,1536]{1,0:T(8,128)(2,1)S(1)} %get-tuple-element.61), channel_id=1, source_target_pairs={{4,0},{6,2},{5,1},{7,3},{8,4},{10,6},{9,5},{11,7},{12,8},{14,10},{... | collective-permute-start | bytes 294920 | tf_op jit(solution)/shard_map/ppermute | solution.py:48
  90.7 3.6 %shard_map.105 = (bf16[1536,1536]{1,0:T(8,128)(2,1)}, f32[1,1536]{1,0:T(1,128)S(1)}) custom-call(bf16[512,768]{1,0:T(8,128)(2,1)S(1)} %shard_map.104.left_own, bf16[512,768]{1,0:T(8,128)(2,1)S(1)} %collective-permute-done.27.left_other, bf16[512,1536]{1,0:T(8,128)(2,1)S(1)} %get-tuple-element.45.refs_4_.right_own, ...), custom_call_target="tpu_custom_call" | custom-call | tf_op jit(solution)/shard_map/pallas_call | solution.py:285
  (76 shorter events, 24.4 us)
Async XLA Ops:
  1.6 7.3 %collective-permute-start = (bf16[2,32,1536]{2,1,0:T(8,128)(2,1)S(1)}, bf16[2,32,1536]{2,1,0:T(8,128)(2,1)S(1)}, u32[]{:S(2)}, u32[]{:S(2)}) collective-permute-start(bf16[2,32,1536]{2,1,0:T(8,128)(2,1)S(1)} %pad_maximum_fusion.refs_3_), channel_id=1, source_target_pairs={{8,0},{10,2},{9,1},{11,3},{12,4},{14,6},{13,5},{15,7},{0,8},{2,10}... | collective-permute-start | bytes 589832 | tf_op jit(solution)/shard_map/ppermute | solution.py:48
  4.8 6.9 %collective-permute-start.1 = (bf16[2,32,1536]{2,1,0:T(8,128)(2,1)S(1)}, bf16[2,32,1536]{2,1,0:T(8,128)(2,1)S(1)}, u32[]{:S(2)}, u32[]{:S(2)}) collective-permute-start(bf16[2,32,1536]{2,1,0:T(8,128)(2,1)S(1)} %pad_maximum_fusion.refs_3_), channel_id=1, source_target_pairs={{12,0},{14,2},{13,1},{15,3},{0,4},{2,6},{1,5},{3,7},{4,8},{6,10},{... | collective-permute-start | bytes 589832 | tf_op jit(solution)/shard_map/ppermute | solution.py:48
  5.4 6.3 %collective-permute-start.2 = (bf16[2,32,1536]{2,1,0:T(8,128)(2,1)S(1)}, bf16[2,32,1536]{2,1,0:T(8,128)(2,1)S(1)}, u32[]{:S(2)}, u32[]{:S(2)}) collective-permute-start(bf16[2,32,1536]{2,1,0:T(8,128)(2,1)S(1)} %pad_maximum_fusion.refs_3_), channel_id=1, source_target_pairs={{4,0},{6,2},{5,1},{7,3},{8,4},{10,6},{9,5},{11,7},{12,8},{14,10},{... | collective-permute-start | bytes 589832 | tf_op jit(solution)/shard_map/ppermute | solution.py:48
  11.7 9.5 %collective-permute-start.6 = (bf16[128,1536]{1,0:T(8,128)(2,1)S(1)}, bf16[128,1536]{1,0:T(8,128)(2,1)S(1)}, u32[]{:S(2)}, u32[]{:S(2)}) collective-permute-start(bf16[128,1536]{1,0:T(8,128)(2,1)S(1)} %get-tuple-element.37.follow.refs_3_), channel_id=1, source_target_pairs={{1,0},{3,2},{0,1},{2,3},{5,4},{7,6},{4,5},{6,7},{9,8},{11,10},{8,9... | collective-permute-start | bytes 1179656 | tf_op jit(solution)/shard_map/ppermute | solution.py:48
  15.0 11.9 %collective-permute-start.7 = (bf16[128,1536]{1,0:T(8,128)(2,1)S(1)}, bf16[128,1536]{1,0:T(8,128)(2,1)S(1)}, u32[]{:S(2)}, u32[]{:S(2)}) collective-permute-start(bf16[128,1536]{1,0:T(8,128)(2,1)S(1)} %get-tuple-element.37.follow.refs_3_), channel_id=1, source_target_pairs={{3,0},{0,2},{2,1},{1,3},{7,4},{4,6},{6,5},{5,7},{11,8},{8,10},{10,... | collective-permute-start | bytes 1179656 | tf_op jit(solution)/shard_map/ppermute | solution.py:48
  15.7 11.2 %collective-permute-start.8 = (bf16[128,1536]{1,0:T(8,128)(2,1)S(1)}, bf16[128,1536]{1,0:T(8,128)(2,1)S(1)}, u32[]{:S(2)}, u32[]{:S(2)}) collective-permute-start(bf16[128,1536]{1,0:T(8,128)(2,1)S(1)} %get-tuple-element.37.follow.refs_3_), channel_id=1, source_target_pairs={{2,0},{1,2},{3,1},{0,3},{6,4},{5,6},{7,5},{4,7},{10,8},{9,10},{11,... | collective-permute-start | bytes 1179656 | tf_op jit(solution)/shard_map/ppermute | solution.py:48
  18.2 11.4 %collective-permute-start.3 = (bf16[128,1536]{1,0:T(8,128)(2,1)S(1)}, bf16[128,1536]{1,0:T(8,128)(2,1)S(1)}, u32[]{:S(2)}, u32[]{:S(2)}) collective-permute-start(bf16[128,1536]{1,0:T(8,128)(2,1)S(1)} %get-tuple-element.36.refs_3_), channel_id=1, source_target_pairs={{1,0},{3,2},{0,1},{2,3},{5,4},{7,6},{4,5},{6,7},{9,8},{11,10},{8,9... | collective-permute-start | bytes 1179656 | tf_op jit(solution)/shard_map/ppermute | solution.py:48
  18.2 15.5 %collective-permute-start.4 = (bf16[128,1536]{1,0:T(8,128)(2,1)S(1)}, bf16[128,1536]{1,0:T(8,128)(2,1)S(1)}, u32[]{:S(2)}, u32[]{:S(2)}) collective-permute-start(bf16[128,1536]{1,0:T(8,128)(2,1)S(1)} %get-tuple-element.36.refs_3_), channel_id=1, source_target_pairs={{3,0},{0,2},{2,1},{1,3},{7,4},{4,6},{6,5},{5,7},{11,8},{8,10},{10,... | collective-permute-start | bytes 1179656 | tf_op jit(solution)/shard_map/ppermute | solution.py:48
  21.2 12.9 %collective-permute-start.5 = (bf16[128,1536]{1,0:T(8,128)(2,1)S(1)}, bf16[128,1536]{1,0:T(8,128)(2,1)S(1)}, u32[]{:S(2)}, u32[]{:S(2)}) collective-permute-start(bf16[128,1536]{1,0:T(8,128)(2,1)S(1)} %get-tuple-element.36.refs_3_), channel_id=1, source_target_pairs={{2,0},{1,2},{3,1},{0,3},{6,4},{5,6},{7,5},{4,7},{10,8},{9,10},{11,... | collective-permute-start | bytes 1179656 | tf_op jit(solution)/shard_map/ppermute | solution.py:48
  35.8 7.9 %collective-permute-start.13 = (bf16[2,128,768]{2,1,0:T(8,128)(2,1)S(1)}, bf16[2,128,768]{2,1,0:T(8,128)(2,1)S(1)}, u32[]{:S(2)}, u32[]{:S(2)}) collective-permute-start(bf16[2,128,768]{2,1,0:T(8,128)(2,1)S(1)} %get-tuple-element.40.refs_5_), channel_id=1, source_target_pairs={{32,0},{34,2},{33,1},{35,3},{36,4},{38,6},{37,5},{39,7},{40,8},{42... | collective-permute-start | bytes 1179656 | tf_op jit(solution)/shard_map/ppermute | solution.py:48
  39.4 9.4 %collective-permute-start.11 = (bf16[2,128,768]{2,1,0:T(8,128)(2,1)S(1)}, bf16[2,128,768]{2,1,0:T(8,128)(2,1)S(1)}, u32[]{:S(2)}, u32[]{:S(2)}) collective-permute-start(bf16[2,128,768]{2,1,0:T(8,128)(2,1)S(1)} %get-tuple-element.43), channel_id=1, source_target_pairs={{32,0},{34,2},{33,1},{35,3},{36,4},{38,6},{37,5},{39,7},{40,8},{42... | collective-permute-start | bytes 1179656 | tf_op jit(solution)/shard_map/ppermute | solution.py:48
  43.7 9.3 %collective-permute-start.14 = (bf16[128,768]{1,0:T(8,128)(2,1)S(1)}, bf16[128,768]{1,0:T(8,128)(2,1)S(1)}, u32[]{:S(2)}, u32[]{:S(2)}) collective-permute-start(bf16[128,768]{1,0:T(8,128)(2,1)S(1)} %get-tuple-element.51), channel_id=1, source_target_pairs={{96,0},{98,2},{97,1},{99,3},{100,4},{102,6},{101,5},{103,7},{104,8... | collective-permute-start | bytes 589832 | tf_op jit(solution)/shard_map/ppermute | solution.py:48
  48.9 9.0 %collective-permute-start.12 = (bf16[128,768]{1,0:T(8,128)(2,1)S(1)}, bf16[128,768]{1,0:T(8,128)(2,1)S(1)}, u32[]{:S(2)}, u32[]{:S(2)}) collective-permute-start(bf16[128,768]{1,0:T(8,128)(2,1)S(1)} %get-tuple-element.47), channel_id=1, source_target_pairs={{96,0},{98,2},{97,1},{99,3},{100,4},{102,6},{101,5},{103,7},{104,8... | collective-permute-start | bytes 589832 | tf_op jit(solution)/shard_map/ppermute | solution.py:48
  53.3 10.5 %collective-permute-start.18 = (bf16[128,768]{1,0:T(8,128)(2,1)S(1)}, bf16[128,768]{1,0:T(8,128)(2,1)S(1)}, u32[]{:S(2)}, u32[]{:S(2)}) collective-permute-start(bf16[128,768]{1,0:T(8,128)(2,1)S(1)} %get-tuple-element.53.refs_0_), channel_id=1, source_target_pairs={{32,0},{34,2},{33,1},{35,3},{36,4},{38,6},{37,5},{39,7},{40,8},{42... | collective-permute-start | bytes 589832 | tf_op jit(solution)/shard_map/ppermute | solution.py:48
  57.9 8.7 %collective-permute-start.15 = (bf16[128,768]{1,0:T(8,128)(2,1)S(1)}, bf16[128,768]{1,0:T(8,128)(2,1)S(1)}, u32[]{:S(2)}, u32[]{:S(2)}) collective-permute-start(bf16[128,768]{1,0:T(8,128)(2,1)S(1)} %shard_map.97.refs_3_), channel_id=1, source_target_pairs={{64,0},{66,2},{65,1},{67,3},{68,4},{70,6},{69,5},{71,7},{72,8},{74... | collective-permute-start | bytes 589832 | tf_op jit(solution)/shard_map/ppermute | solution.py:48
  60.6 7.9 %collective-permute-start.16 = (bf16[128,768]{1,0:T(8,128)(2,1)S(1)}, bf16[128,768]{1,0:T(8,128)(2,1)S(1)}, u32[]{:S(2)}, u32[]{:S(2)}) collective-permute-start(bf16[128,768]{1,0:T(8,128)(2,1)S(1)} %shard_map.97.refs_3_), channel_id=1, source_target_pairs={{96,0},{98,2},{97,1},{99,3},{100,4},{102,6},{101,5},{103,7},{104,8... | collective-permute-start | bytes 589832 | tf_op jit(solution)/shard_map/ppermute | solution.py:48
  62.5 6.0 %collective-permute-start.17 = (bf16[128,768]{1,0:T(8,128)(2,1)S(1)}, bf16[128,768]{1,0:T(8,128)(2,1)S(1)}, u32[]{:S(2)}, u32[]{:S(2)}) collective-permute-start(bf16[128,768]{1,0:T(8,128)(2,1)S(1)} %shard_map.97.refs_3_), channel_id=1, source_target_pairs={{32,0},{34,2},{33,1},{35,3},{36,4},{38,6},{37,5},{39,7},{40,8},{42... | collective-permute-start | bytes 589832 | tf_op jit(solution)/shard_map/ppermute | solution.py:48
  72.5 11.5 %collective-permute-start.20 = (bf16[128,1536]{1,0:T(8,128)(2,1)S(1)}, bf16[128,1536]{1,0:T(8,128)(2,1)S(1)}, u32[]{:S(2)}, u32[]{:S(2)}) collective-permute-start(bf16[128,1536]{1,0:T(8,128)(2,1)S(1)} %get-tuple-element.54), channel_id=1, source_target_pairs={{1,0},{3,2},{0,1},{2,3},{5,4},{7,6},{4,5},{6,7},{9,8},{11,10},{8,9... | collective-permute-start | bytes 1179656 | tf_op jit(solution)/shard_map/ppermute | solution.py:48
  74.7 11.4 %collective-permute-start.21 = (bf16[128,1536]{1,0:T(8,128)(2,1)S(1)}, bf16[128,1536]{1,0:T(8,128)(2,1)S(1)}, u32[]{:S(2)}, u32[]{:S(2)}) collective-permute-start(bf16[128,1536]{1,0:T(8,128)(2,1)S(1)} %get-tuple-element.55), channel_id=1, source_target_pairs={{2,0},{1,2},{3,1},{0,3},{6,4},{5,6},{7,5},{4,7},{10,8},{9,10},{11,... | collective-permute-start | bytes 1179656 | tf_op jit(solution)/shard_map/ppermute | solution.py:48
  76.7 9.4 %collective-permute-start.22 = (bf16[128,1536]{1,0:T(8,128)(2,1)S(1)}, bf16[128,1536]{1,0:T(8,128)(2,1)S(1)}, u32[]{:S(2)}, u32[]{:S(2)}) collective-permute-start(bf16[128,1536]{1,0:T(8,128)(2,1)S(1)} %get-tuple-element.56.refs_0_), channel_id=1, source_target_pairs={{3,0},{0,2},{2,1},{1,3},{7,4},{4,6},{6,5},{5,7},{11,8},{8,10},{10,... | collective-permute-start | bytes 1179656 | tf_op jit(solution)/shard_map/ppermute | solution.py:48
  76.8 9.5 %collective-permute-start.26 = (bf16[2,128,768]{2,1,0:T(8,128)(2,1)S(1)}, bf16[2,128,768]{2,1,0:T(8,128)(2,1)S(1)}, u32[]{:S(2)}, u32[]{:S(2)}) collective-permute-start(bf16[2,128,768]{2,1,0:T(8,128)(2,1)S(1)} %shard_map.103), channel_id=1, source_target_pairs={{96,0},{98,2},{97,1},{99,3},{100,4},{102,6},{101,5},{103,7},{104,8... | collective-permute-start | bytes 1179656 | tf_op jit(solution)/shard_map/ppermute | solution.py:48
  86.5 7.8 %collective-permute-start.23 = (bf16[32,1536]{1,0:T(8,128)(2,1)S(1)}, bf16[32,1536]{1,0:T(8,128)(2,1)S(1)}, u32[]{:S(2)}, u32[]{:S(2)}) collective-permute-start(bf16[32,1536]{1,0:T(8,128)(2,1)S(1)} %get-tuple-element.60), channel_id=1, source_target_pairs={{8,0},{10,2},{9,1},{11,3},{12,4},{14,6},{13,5},{15,7},{0,8},{2,10}... | collective-permute-start | bytes 294920 | tf_op jit(solution)/shard_map/ppermute | solution.py:48
  88.1 6.2 %collective-permute-start.24 = (bf16[32,1536]{1,0:T(8,128)(2,1)S(1)}, bf16[32,1536]{1,0:T(8,128)(2,1)S(1)}, u32[]{:S(2)}, u32[]{:S(2)}) collective-permute-start(bf16[32,1536]{1,0:T(8,128)(2,1)S(1)} %get-tuple-element.61), channel_id=1, source_target_pairs={{4,0},{6,2},{5,1},{7,3},{8,4},{10,6},{9,5},{11,7},{12,8},{14,10},{... | collective-permute-start | bytes 294920 | tf_op jit(solution)/shard_map/ppermute | solution.py:48
  90.2 5.8 %collective-permute-start.25 = (bf16[32,1536]{1,0:T(8,128)(2,1)S(1)}, bf16[32,1536]{1,0:T(8,128)(2,1)S(1)}, u32[]{:S(2)}, u32[]{:S(2)}) collective-permute-start(bf16[32,1536]{1,0:T(8,128)(2,1)S(1)} %get-tuple-element.62), channel_id=1, source_target_pairs={{12,0},{14,2},{13,1},{15,3},{0,4},{2,6},{1,5},{3,7},{4,8},{6,10},{... | collective-permute-start | bytes 294920 | tf_op jit(solution)/shard_map/ppermute | solution.py:48
  (12 other events, 78.0 us)

commit v2 on v1

--- a/solution.py
+++ b/solution.py
@@ -83,6 +83,25 @@
 
 def swapped_rows(ref, block, tokens):
     return jnp.concatenate([ref[span(a * 4 + block, tokens), :] for a in range(4)], axis=0)
+
+
+def stack_kernel(first, second, out, done):
+    copies = [pltpu.make_async_copy(ref, out.at[i], done.at[i]) for i, ref in enumerate((first, second))]
+    for copy in copies:
+        copy.start()
+    for copy in copies:
+        copy.wait()
+
+
+def stacked(first, second):
+    return pl.pallas_call(
+        stack_kernel,
+        out_shape=pltpu.VMEM((2,) + first.shape, first.dtype),
+        in_specs=[pl.BlockSpec(memory_space=pltpu.HBM)] * 2,
+        out_specs=pl.BlockSpec(memory_space=pltpu.VMEM),
+        scratch_shapes=[pltpu.SemaphoreType.DMA((2,))],
+        compiler_params=pltpu.CompilerParams(vmem_limit_bytes=48 * MIB),
+    )(first, second)
 
 
 def line_kernel(last, far, near, mine, ins, grads):
@@ -303,7 +322,7 @@
     hidden = w_in.shape[1]
     half, every, line = hidden // 2, 16 * tokens, 4 * tokens
 
-    mine = jnp.stack([inputs, out_grad])
+    mine = stacked(inputs, out_grad)
     steps = ring(mine, along_first)
     ins, grads = local(line_kernel, [((line, features), BF16)] * 2, steps[::-1] + [mine])
     ins = [ins] + ring(ins, along_second)

time: 97.3 us -> 98.4 us (1.011)
  local copies, waits for them, and re-layouts: 2.38 us -> 4.16 us
    unnamed x16 -> x20, local copies, waits for them, and re-layouts: 2.37 us -> 4.15 us
where the time goes in v2:
time: 98.4 us; the launch traced here: 97.8 us
  starting transfers between devices  45.2 us (46%)
  waiting for transfers between devices  27.9 us (28%)
  Pallas kernels  19.5 us (20%)
  local copies, waits for them, and re-layouts  4.16 us (4%)
  between operations  0.99 us (1%)
    ppermute x28, starting transfers between devices, send(): return lax.ppermute(value, AXES, perm)  45.2 us
    ppermute x28, waiting for transfers between devices, send(): return lax.ppermute(value, AXES, perm)  27.9 us
    pallas_call x20, Pallas kernels, local(): pl.pallas_call(run, out_shape=[result(shape, dtype) for shape, dtype in o...  10.6 us
    pallas_call x2, Pallas kernels, grad_of(): pl.pallas_call(functools.partial(grad_kernel, to_columns), out_shape=[jax...  8.32 us
    unnamed x20, local copies, waits for them, and re-layouts  4.15 us
  transfers between devices with their start and end apart: 28, of which 13 were waited for; matrix products, arithmetic and copies ran while one was open for 0% of the time, Pallas kernels for 16%

profile of v2, /device:TPU:0, one launch (start us, length us, event | category | flops | bytes accessed | tf_op | source)
XLA Modules:
  0.0 97.8 jit_solution(15175595324776657156)
XLA Ops:
  2.7 3.2 %collective-permute-start = (bf16[2,32,1536]{2,1,0:T(8,128)(2,1)S(1)}, bf16[2,32,1536]{2,1,0:T(8,128)(2,1)S(1)}, u32[]{:S(2)}, u32[]{:S(2)}) collective-permute-start(bf16[2,32,1536]{2,1,0:T(8,128)(2,1)S(1)} %shard_map.84.refs_3_), channel_id=1, source_target_pairs={{8,0},{10,2},{9,1},{11,3},{12,4},{14,6},{13,5},{15,7},{0,8},{2,10}... | collective-permute-start | bytes 589832 | tf_op jit(solution)/shard_map/ppermute | solution.py:48
  6.4 2.6 %collective-permute-start.2 = (bf16[2,32,1536]{2,1,0:T(8,128)(2,1)S(1)}, bf16[2,32,1536]{2,1,0:T(8,128)(2,1)S(1)}, u32[]{:S(2)}, u32[]{:S(2)}) collective-permute-start(bf16[2,32,1536]{2,1,0:T(8,128)(2,1)S(1)} %shard_map.84.refs_3_), channel_id=1, source_target_pairs={{4,0},{6,2},{5,1},{7,3},{8,4},{10,6},{9,5},{11,7},{12,8},{14,10},{... | collective-permute-start | bytes 589832 | tf_op jit(solution)/shard_map/ppermute | solution.py:48
  9.9 2.8 %collective-permute-done.1.refs_1_ = bf16[2,32,1536]{2,1,0:T(8,128)(2,1)S(1)} collective-permute-done((bf16[2,32,1536]{2,1,0:T(8,128)(2,1)S(1)}, bf16[2,32,1536]{2,1,0:T(8,128)(2,1)S(1)}, u32[]{:S(2)}, u32[]{:S(2)}) %collective-permute-start.1) | collective-permute-done | bytes 196640 | tf_op jit(solution)/shard_map/ppermute | solution.py:48
  12.8 3.3 %collective-permute-start.6 = (bf16[128,1536]{1,0:T(8,128)(2,1)S(1)}, bf16[128,1536]{1,0:T(8,128)(2,1)S(1)}, u32[]{:S(2)}, u32[]{:S(2)}) collective-permute-start(bf16[128,1536]{1,0:T(8,128)(2,1)S(1)} %get-tuple-element.37.follow.refs_3_), channel_id=1, source_target_pairs={{1,0},{3,2},{0,1},{2,3},{5,4},{7,6},{4,5},{6,7},{9,8},{11,10},{8,9... | collective-permute-start | bytes 1179656 | tf_op jit(solution)/shard_map/ppermute | solution.py:48
  16.7 2.6 %collective-permute-start.8 = (bf16[128,1536]{1,0:T(8,128)(2,1)S(1)}, bf16[128,1536]{1,0:T(8,128)(2,1)S(1)}, u32[]{:S(2)}, u32[]{:S(2)}) collective-permute-start(bf16[128,1536]{1,0:T(8,128)(2,1)S(1)} %get-tuple-element.37.follow.refs_3_), channel_id=1, source_target_pairs={{2,0},{1,2},{3,1},{0,3},{6,4},{5,6},{7,5},{4,7},{10,8},{9,10},{11,... | collective-permute-start | bytes 1179656 | tf_op jit(solution)/shard_map/ppermute | solution.py:48
  20.2 2.1 %collective-permute-done.6.refs_0_ = bf16[128,1536]{1,0:T(8,128)(2,1)S(1)} collective-permute-done((bf16[128,1536]{1,0:T(8,128)(2,1)S(1)}, bf16[128,1536]{1,0:T(8,128)(2,1)S(1)}, u32[]{:S(2)}, u32[]{:S(2)}) %collective-permute-start.6) | collective-permute-done | bytes 393248 | tf_op jit(solution)/shard_map/ppermute | solution.py:48
  22.3 3.0 %collective-permute-start.5 = (bf16[128,1536]{1,0:T(8,128)(2,1)S(1)}, bf16[128,1536]{1,0:T(8,128)(2,1)S(1)}, u32[]{:S(2)}, u32[]{:S(2)}) collective-permute-start(bf16[128,1536]{1,0:T(8,128)(2,1)S(1)} %get-tuple-element.36.refs_3_), channel_id=1, source_target_pairs={{2,0},{1,2},{3,1},{0,3},{6,4},{5,6},{7,5},{4,7},{10,8},{9,10},{11,... | collective-permute-start | bytes 1179656 | tf_op jit(solution)/shard_map/ppermute | solution.py:48
  25.3 2.3 %copy-done.1 = bf16[1536,1536]{1,0:T(8,128)(2,1)S(1)} copy-done((bf16[1536,1536]{1,0:T(8,128)(2,1)S(1)}, bf16[1536,1536]{1,0:T(8,128)(2,1)}, u32[]{:S(2)}) %copy-start.1) | copy-done | bytes 4718616
  28.0 2.6 %shard_map.88 = (bf16[512,768]{1,0:T(8,128)(2,1)S(1)}, f32[512,768]{1,0:T(8,128)S(1)}) custom-call(bf16[128,1536]{1,0:T(8,128)(2,1)S(1)} %collective-permute-done.6.refs_0_, bf16[128,1536]{1,0:T(8,128)(2,1)S(1)} %collective-permute-done.7.refs_1_, bf16[128,1536]{1,0:T(8,128)(2,1)S(1)} %collective-permute-done.8.refs_2_, ...), custom_call_target="tpu_custom_call" | custom-call | tf_op jit(solution)/shard_map/pallas_call | solution.py:64
  30.7 4.0 %collective-permute-done.4.refs_1_ = bf16[128,1536]{1,0:T(8,128)(2,1)S(1)} collective-permute-done((bf16[128,1536]{1,0:T(8,128)(2,1)S(1)}, bf16[128,1536]{1,0:T(8,128)(2,1)S(1)}, u32[]{:S(2)}, u32[]{:S(2)}) %collective-permute-start.4) | collective-permute-done | bytes 393248 | tf_op jit(solution)/shard_map/ppermute | solution.py:48
  36.9 2.0 %collective-permute-start.13 = (bf16[2,128,768]{2,1,0:T(8,128)(2,1)S(1)}, bf16[2,128,768]{2,1,0:T(8,128)(2,1)S(1)}, u32[]{:S(2)}, u32[]{:S(2)}) collective-permute-start(bf16[2,128,768]{2,1,0:T(8,128)(2,1)S(1)} %get-tuple-element.40.refs_5_), channel_id=1, source_target_pairs={{32,0},{34,2},{33,1},{35,3},{36,4},{38,6},{37,5},{39,7},{40,8},{42... | collective-permute-start | bytes 1179656 | tf_op jit(solution)/shard_map/ppermute | solution.py:48
  41.3 3.5 %collective-permute-done.13.refs_2_ = bf16[2,128,768]{2,1,0:T(8,128)(2,1)S(1)} collective-permute-done((bf16[2,128,768]{2,1,0:T(8,128)(2,1)S(1)}, bf16[2,128,768]{2,1,0:T(8,128)(2,1)S(1)}, u32[]{:S(2)}, u32[]{:S(2)}) %collective-permute-start.13) | collective-permute-done | bytes 393248 | tf_op jit(solution)/shard_map/ppermute | solution.py:48
  44.8 4.1 %collective-permute-start.14 = (bf16[128,768]{1,0:T(8,128)(2,1)S(1)}, bf16[128,768]{1,0:T(8,128)(2,1)S(1)}, u32[]{:S(2)}, u32[]{:S(2)}) collective-permute-start(bf16[128,768]{1,0:T(8,128)(2,1)S(1)} %get-tuple-element.51), channel_id=1, source_target_pairs={{96,0},{98,2},{97,1},{99,3},{100,4},{102,6},{101,5},{103,7},{104,8... | collective-permute-start | bytes 589832 | tf_op jit(solution)/shard_map/ppermute | solution.py:48
  49.9 4.1 %collective-permute-start.12 = (bf16[128,768]{1,0:T(8,128)(2,1)S(1)}, bf16[128,768]{1,0:T(8,128)(2,1)S(1)}, u32[]{:S(2)}, u32[]{:S(2)}) collective-permute-start(bf16[128,768]{1,0:T(8,128)(2,1)S(1)} %get-tuple-element.47), channel_id=1, source_target_pairs={{96,0},{98,2},{97,1},{99,3},{100,4},{102,6},{101,5},{103,7},{104,8... | collective-permute-start | bytes 589832 | tf_op jit(solution)/shard_map/ppermute | solution.py:48
  54.5 4.5 %collective-permute-done.12.refs_1_ = bf16[128,768]{1,0:T(8,128)(2,1)S(1)} collective-permute-done((bf16[128,768]{1,0:T(8,128)(2,1)S(1)}, bf16[128,768]{1,0:T(8,128)(2,1)S(1)}, u32[]{:S(2)}, u32[]{:S(2)}) %collective-permute-start.12) | collective-permute-done | bytes 196640 | tf_op jit(solution)/shard_map/ppermute | solution.py:48
  59.0 2.6 %collective-permute-start.15 = (bf16[128,768]{1,0:T(8,128)(2,1)S(1)}, bf16[128,768]{1,0:T(8,128)(2,1)S(1)}, u32[]{:S(2)}, u32[]{:S(2)}) collective-permute-start(bf16[128,768]{1,0:T(8,128)(2,1)S(1)} %shard_map.98.refs_3_), channel_id=1, source_target_pairs={{64,0},{66,2},{65,1},{67,3},{68,4},{70,6},{69,5},{71,7},{72,8},{74... | collective-permute-start | bytes 589832 | tf_op jit(solution)/shard_map/ppermute | solution.py:48
  64.9 2.8 %collective-permute-done.15.refs_0_ = bf16[128,768]{1,0:T(8,128)(2,1)S(1)} collective-permute-done((bf16[128,768]{1,0:T(8,128)(2,1)S(1)}, bf16[128,768]{1,0:T(8,128)(2,1)S(1)}, u32[]{:S(2)}, u32[]{:S(2)}) %collective-permute-start.15) | collective-permute-done | bytes 196640 | tf_op jit(solution)/shard_map/ppermute | solution.py:48
  73.6 2.2 %collective-permute-start.20 = (bf16[128,1536]{1,0:T(8,128)(2,1)S(1)}, bf16[128,1536]{1,0:T(8,128)(2,1)S(1)}, u32[]{:S(2)}, u32[]{:S(2)}) collective-permute-start(bf16[128,1536]{1,0:T(8,128)(2,1)S(1)} %get-tuple-element.54), channel_id=1, source_target_pairs={{1,0},{3,2},{0,1},{2,3},{5,4},{7,6},{4,5},{6,7},{9,8},{11,10},{8,9... | collective-permute-start | bytes 1179656 | tf_op jit(solution)/shard_map/ppermute | solution.py:48
  75.8 2.0 %collective-permute-start.21 = (bf16[128,1536]{1,0:T(8,128)(2,1)S(1)}, bf16[128,1536]{1,0:T(8,128)(2,1)S(1)}, u32[]{:S(2)}, u32[]{:S(2)}) collective-permute-start(bf16[128,1536]{1,0:T(8,128)(2,1)S(1)} %get-tuple-element.55), channel_id=1, source_target_pairs={{2,0},{1,2},{3,1},{0,3},{6,4},{5,6},{7,5},{4,7},{10,8},{9,10},{11,... | collective-permute-start | bytes 1179656 | tf_op jit(solution)/shard_map/ppermute | solution.py:48
  77.8 2.5 %collective-permute-start.26 = (bf16[2,128,768]{2,1,0:T(8,128)(2,1)S(1)}, bf16[2,128,768]{2,1,0:T(8,128)(2,1)S(1)}, u32[]{:S(2)}, u32[]{:S(2)}) collective-permute-start(bf16[2,128,768]{2,1,0:T(8,128)(2,1)S(1)} %shard_map.104), channel_id=1, source_target_pairs={{96,0},{98,2},{97,1},{99,3},{100,4},{102,6},{101,5},{103,7},{104,8... | collective-permute-start | bytes 1179656 | tf_op jit(solution)/shard_map/ppermute | solution.py:48
  80.3 4.7 %shard_map.102 = (bf16[1536,1536]{1,0:T(8,128)(2,1)}, f32[1,1536]{1,0:T(1,128)S(1)}) custom-call(bf16[512,1536]{1,0:T(8,128)(2,1)S(1)} %get-tuple-element.44.refs_3_.left_own, bf16[512,1536]{1,0:T(8,128)(2,1)S(1)} %get-tuple-element.58.left_other, bf16[512,768]{1,0:T(8,128)(2,1)S(1)} %shard_map.99.refs_0_.right_own, ...), custom_call_target="tpu_custom_call" | custom-call | tf_op jit(solution)/shard_map/pallas_call | solution.py:304
  85.1 2.0 %collective-permute-done.21.refs_1_ = bf16[128,1536]{1,0:T(8,128)(2,1)S(1)} collective-permute-done((bf16[128,1536]{1,0:T(8,128)(2,1)S(1)}, bf16[128,1536]{1,0:T(8,128)(2,1)S(1)}, u32[]{:S(2)}, u32[]{:S(2)}) %collective-permute-start.21) | collective-permute-done | bytes 393248 | tf_op jit(solution)/shard_map/ppermute | solution.py:48
  89.2 2.1 %collective-permute-start.24 = (bf16[32,1536]{1,0:T(8,128)(2,1)S(1)}, bf16[32,1536]{1,0:T(8,128)(2,1)S(1)}, u32[]{:S(2)}, u32[]{:S(2)}) collective-permute-start(bf16[32,1536]{1,0:T(8,128)(2,1)S(1)} %get-tuple-element.61), channel_id=1, source_target_pairs={{4,0},{6,2},{5,1},{7,3},{8,4},{10,6},{9,5},{11,7},{12,8},{14,10},{... | collective-permute-start | bytes 294920 | tf_op jit(solution)/shard_map/ppermute | solution.py:48
  91.7 3.6 %shard_map.106 = (bf16[1536,1536]{1,0:T(8,128)(2,1)}, f32[1,1536]{1,0:T(1,128)S(1)}) custom-call(bf16[512,768]{1,0:T(8,128)(2,1)S(1)} %shard_map.105.left_own, bf16[512,768]{1,0:T(8,128)(2,1)S(1)} %collective-permute-done.27.left_other, bf16[512,1536]{1,0:T(8,128)(2,1)S(1)} %get-tuple-element.45.refs_4_.right_own, ...), custom_call_target="tpu_custom_call" | custom-call | tf_op jit(solution)/shard_map/pallas_call | solution.py:304
  (80 shorter events, 25.4 us)
Async XLA Ops:
  2.7 7.3 %collective-permute-start = (bf16[2,32,1536]{2,1,0:T(8,128)(2,1)S(1)}, bf16[2,32,1536]{2,1,0:T(8,128)(2,1)S(1)}, u32[]{:S(2)}, u32[]{:S(2)}) collective-permute-start(bf16[2,32,1536]{2,1,0:T(8,128)(2,1)S(1)} %shard_map.84.refs_3_), channel_id=1, source_target_pairs={{8,0},{10,2},{9,1},{11,3},{12,4},{14,6},{13,5},{15,7},{0,8},{2,10}... | collective-permute-start | bytes 589832 | tf_op jit(solution)/shard_map/ppermute | solution.py:48
  5.9 6.9 %collective-permute-start.1 = (bf16[2,32,1536]{2,1,0:T(8,128)(2,1)S(1)}, bf16[2,32,1536]{2,1,0:T(8,128)(2,1)S(1)}, u32[]{:S(2)}, u32[]{:S(2)}) collective-permute-start(bf16[2,32,1536]{2,1,0:T(8,128)(2,1)S(1)} %shard_map.84.refs_3_), channel_id=1, source_target_pairs={{12,0},{14,2},{13,1},{15,3},{0,4},{2,6},{1,5},{3,7},{4,8},{6,10},{... | collective-permute-start | bytes 589832 | tf_op jit(solution)/shard_map/ppermute | solution.py:48
  6.4 6.3 %collective-permute-start.2 = (bf16[2,32,1536]{2,1,0:T(8,128)(2,1)S(1)}, bf16[2,32,1536]{2,1,0:T(8,128)(2,1)S(1)}, u32[]{:S(2)}, u32[]{:S(2)}) collective-permute-start(bf16[2,32,1536]{2,1,0:T(8,128)(2,1)S(1)} %shard_map.84.refs_3_), channel_id=1, source_target_pairs={{4,0},{6,2},{5,1},{7,3},{8,4},{10,6},{9,5},{11,7},{12,8},{14,10},{... | collective-permute-start | bytes 589832 | tf_op jit(solution)/shard_map/ppermute | solution.py:48
  12.8 9.5 %collective-permute-start.6 = (bf16[128,1536]{1,0:T(8,128)(2,1)S(1)}, bf16[128,1536]{1,0:T(8,128)(2,1)S(1)}, u32[]{:S(2)}, u32[]{:S(2)}) collective-permute-start(bf16[128,1536]{1,0:T(8,128)(2,1)S(1)} %get-tuple-element.37.follow.refs_3_), channel_id=1, source_target_pairs={{1,0},{3,2},{0,1},{2,3},{5,4},{7,6},{4,5},{6,7},{9,8},{11,10},{8,9... | collective-permute-start | bytes 1179656 | tf_op jit(solution)/shard_map/ppermute | solution.py:48
  16.1 11.9 %collective-permute-start.7 = (bf16[128,1536]{1,0:T(8,128)(2,1)S(1)}, bf16[128,1536]{1,0:T(8,128)(2,1)S(1)}, u32[]{:S(2)}, u32[]{:S(2)}) collective-permute-start(bf16[128,1536]{1,0:T(8,128)(2,1)S(1)} %get-tuple-element.37.follow.refs_3_), channel_id=1, source_target_pairs={{3,0},{0,2},{2,1},{1,3},{7,4},{4,6},{6,5},{5,7},{11,8},{8,10},{10,... | collective-permute-start | bytes 1179656 | tf_op jit(solution)/shard_map/ppermute | solution.py:48
  16.7 11.2 %collective-permute-start.8 = (bf16[128,1536]{1,0:T(8,128)(2,1)S(1)}, bf16[128,1536]{1,0:T(8,128)(2,1)S(1)}, u32[]{:S(2)}, u32[]{:S(2)}) collective-permute-start(bf16[128,1536]{1,0:T(8,128)(2,1)S(1)} %get-tuple-element.37.follow.refs_3_), channel_id=1, source_target_pairs={{2,0},{1,2},{3,1},{0,3},{6,4},{5,6},{7,5},{4,7},{10,8},{9,10},{11,... | collective-permute-start | bytes 1179656 | tf_op jit(solution)/shard_map/ppermute | solution.py:48
  19.3 11.4 %collective-permute-start.3 = (bf16[128,1536]{1,0:T(8,128)(2,1)S(1)}, bf16[128,1536]{1,0:T(8,128)(2,1)S(1)}, u32[]{:S(2)}, u32[]{:S(2)}) collective-permute-start(bf16[128,1536]{1,0:T(8,128)(2,1)S(1)} %get-tuple-element.36.refs_3_), channel_id=1, source_target_pairs={{1,0},{3,2},{0,1},{2,3},{5,4},{7,6},{4,5},{6,7},{9,8},{11,10},{8,9... | collective-permute-start | bytes 1179656 | tf_op jit(solution)/shard_map/ppermute | solution.py:48
  19.3 15.5 %collective-permute-start.4 = (bf16[128,1536]{1,0:T(8,128)(2,1)S(1)}, bf16[128,1536]{1,0:T(8,128)(2,1)S(1)}, u32[]{:S(2)}, u32[]{:S(2)}) collective-permute-start(bf16[128,1536]{1,0:T(8,128)(2,1)S(1)} %get-tuple-element.36.refs_3_), channel_id=1, source_target_pairs={{3,0},{0,2},{2,1},{1,3},{7,4},{4,6},{6,5},{5,7},{11,8},{8,10},{10,... | collective-permute-start | bytes 1179656 | tf_op jit(solution)/shard_map/ppermute | solution.py:48
  22.3 12.9 %collective-permute-start.5 = (bf16[128,1536]{1,0:T(8,128)(2,1)S(1)}, bf16[128,1536]{1,0:T(8,128)(2,1)S(1)}, u32[]{:S(2)}, u32[]{:S(2)}) collective-permute-start(bf16[128,1536]{1,0:T(8,128)(2,1)S(1)} %get-tuple-element.36.refs_3_), channel_id=1, source_target_pairs={{2,0},{1,2},{3,1},{0,3},{6,4},{5,6},{7,5},{4,7},{10,8},{9,10},{11,... | collective-permute-start | bytes 1179656 | tf_op jit(solution)/shard_map/ppermute | solution.py:48
  36.9 7.9 %collective-permute-start.13 = (bf16[2,128,768]{2,1,0:T(8,128)(2,1)S(1)}, bf16[2,128,768]{2,1,0:T(8,128)(2,1)S(1)}, u32[]{:S(2)}, u32[]{:S(2)}) collective-permute-start(bf16[2,128,768]{2,1,0:T(8,128)(2,1)S(1)} %get-tuple-element.40.refs_5_), channel_id=1, source_target_pairs={{32,0},{34,2},{33,1},{35,3},{36,4},{38,6},{37,5},{39,7},{40,8},{42... | collective-permute-start | bytes 1179656 | tf_op jit(solution)/shard_map/ppermute | solution.py:48
  40.5 9.4 %collective-permute-start.11 = (bf16[2,128,768]{2,1,0:T(8,128)(2,1)S(1)}, bf16[2,128,768]{2,1,0:T(8,128)(2,1)S(1)}, u32[]{:S(2)}, u32[]{:S(2)}) collective-permute-start(bf16[2,128,768]{2,1,0:T(8,128)(2,1)S(1)} %get-tuple-element.43), channel_id=1, source_target_pairs={{32,0},{34,2},{33,1},{35,3},{36,4},{38,6},{37,5},{39,7},{40,8},{42... | collective-permute-start | bytes 1179656 | tf_op jit(solution)/shard_map/ppermute | solution.py:48
  44.8 9.3 %collective-permute-start.14 = (bf16[128,768]{1,0:T(8,128)(2,1)S(1)}, bf16[128,768]{1,0:T(8,128)(2,1)S(1)}, u32[]{:S(2)}, u32[]{:S(2)}) collective-permute-start(bf16[128,768]{1,0:T(8,128)(2,1)S(1)} %get-tuple-element.51), channel_id=1, source_target_pairs={{96,0},{98,2},{97,1},{99,3},{100,4},{102,6},{101,5},{103,7},{104,8... | collective-permute-start | bytes 589832 | tf_op jit(solution)/shard_map/ppermute | solution.py:48
  49.9 9.1 %collective-permute-start.12 = (bf16[128,768]{1,0:T(8,128)(2,1)S(1)}, bf16[128,768]{1,0:T(8,128)(2,1)S(1)}, u32[]{:S(2)}, u32[]{:S(2)}) collective-permute-start(bf16[128,768]{1,0:T(8,128)(2,1)S(1)} %get-tuple-element.47), channel_id=1, source_target_pairs={{96,0},{98,2},{97,1},{99,3},{100,4},{102,6},{101,5},{103,7},{104,8... | collective-permute-start | bytes 589832 | tf_op jit(solution)/shard_map/ppermute | solution.py:48
  54.4 10.5 %collective-permute-start.18 = (bf16[128,768]{1,0:T(8,128)(2,1)S(1)}, bf16[128,768]{1,0:T(8,128)(2,1)S(1)}, u32[]{:S(2)}, u32[]{:S(2)}) collective-permute-start(bf16[128,768]{1,0:T(8,128)(2,1)S(1)} %get-tuple-element.53.refs_0_), channel_id=1, source_target_pairs={{32,0},{34,2},{33,1},{35,3},{36,4},{38,6},{37,5},{39,7},{40,8},{42... | collective-permute-start | bytes 589832 | tf_op jit(solution)/shard_map/ppermute | solution.py:48
  59.0 8.7 %collective-permute-start.15 = (bf16[128,768]{1,0:T(8,128)(2,1)S(1)}, bf16[128,768]{1,0:T(8,128)(2,1)S(1)}, u32[]{:S(2)}, u32[]{:S(2)}) collective-permute-start(bf16[128,768]{1,0:T(8,128)(2,1)S(1)} %shard_map.98.refs_3_), channel_id=1, source_target_pairs={{64,0},{66,2},{65,1},{67,3},{68,4},{70,6},{69,5},{71,7},{72,8},{74... | collective-permute-start | bytes 589832 | tf_op jit(solution)/shard_map/ppermute | solution.py:48
  61.6 7.9 %collective-permute-start.16 = (bf16[128,768]{1,0:T(8,128)(2,1)S(1)}, bf16[128,768]{1,0:T(8,128)(2,1)S(1)}, u32[]{:S(2)}, u32[]{:S(2)}) collective-permute-start(bf16[128,768]{1,0:T(8,128)(2,1)S(1)} %shard_map.98.refs_3_), channel_id=1, source_target_pairs={{96,0},{98,2},{97,1},{99,3},{100,4},{102,6},{101,5},{103,7},{104,8... | collective-permute-start | bytes 589832 | tf_op jit(solution)/shard_map/ppermute | solution.py:48
  63.6 6.0 %collective-permute-start.17 = (bf16[128,768]{1,0:T(8,128)(2,1)S(1)}, bf16[128,768]{1,0:T(8,128)(2,1)S(1)}, u32[]{:S(2)}, u32[]{:S(2)}) collective-permute-start(bf16[128,768]{1,0:T(8,128)(2,1)S(1)} %shard_map.98.refs_3_), channel_id=1, source_target_pairs={{32,0},{34,2},{33,1},{35,3},{36,4},{38,6},{37,5},{39,7},{40,8},{42... | collective-permute-start | bytes 589832 | tf_op jit(solution)/shard_map/ppermute | solution.py:48
  73.6 11.5 %collective-permute-start.20 = (bf16[128,1536]{1,0:T(8,128)(2,1)S(1)}, bf16[128,1536]{1,0:T(8,128)(2,1)S(1)}, u32[]{:S(2)}, u32[]{:S(2)}) collective-permute-start(bf16[128,1536]{1,0:T(8,128)(2,1)S(1)} %get-tuple-element.54), channel_id=1, source_target_pairs={{1,0},{3,2},{0,1},{2,3},{5,4},{7,6},{4,5},{6,7},{9,8},{11,10},{8,9... | collective-permute-start | bytes 1179656 | tf_op jit(solution)/shard_map/ppermute | solution.py:48
  75.8 11.4 %collective-permute-start.21 = (bf16[128,1536]{1,0:T(8,128)(2,1)S(1)}, bf16[128,1536]{1,0:T(8,128)(2,1)S(1)}, u32[]{:S(2)}, u32[]{:S(2)}) collective-permute-start(bf16[128,1536]{1,0:T(8,128)(2,1)S(1)} %get-tuple-element.55), channel_id=1, source_target_pairs={{2,0},{1,2},{3,1},{0,3},{6,4},{5,6},{7,5},{4,7},{10,8},{9,10},{11,... | collective-permute-start | bytes 1179656 | tf_op jit(solution)/shard_map/ppermute | solution.py:48
  77.8 9.4 %collective-permute-start.22 = (bf16[128,1536]{1,0:T(8,128)(2,1)S(1)}, bf16[128,1536]{1,0:T(8,128)(2,1)S(1)}, u32[]{:S(2)}, u32[]{:S(2)}) collective-permute-start(bf16[128,1536]{1,0:T(8,128)(2,1)S(1)} %get-tuple-element.56.refs_0_), channel_id=1, source_target_pairs={{3,0},{0,2},{2,1},{1,3},{7,4},{4,6},{6,5},{5,7},{11,8},{8,10},{10,... | collective-permute-start | bytes 1179656 | tf_op jit(solution)/shard_map/ppermute | solution.py:48
  77.8 9.5 %collective-permute-start.26 = (bf16[2,128,768]{2,1,0:T(8,128)(2,1)S(1)}, bf16[2,128,768]{2,1,0:T(8,128)(2,1)S(1)}, u32[]{:S(2)}, u32[]{:S(2)}) collective-permute-start(bf16[2,128,768]{2,1,0:T(8,128)(2,1)S(1)} %shard_map.104), channel_id=1, source_target_pairs={{96,0},{98,2},{97,1},{99,3},{100,4},{102,6},{101,5},{103,7},{104,8... | collective-permute-start | bytes 1179656 | tf_op jit(solution)/shard_map/ppermute | solution.py:48
  87.6 7.8 %collective-permute-start.23 = (bf16[32,1536]{1,0:T(8,128)(2,1)S(1)}, bf16[32,1536]{1,0:T(8,128)(2,1)S(1)}, u32[]{:S(2)}, u32[]{:S(2)}) collective-permute-start(bf16[32,1536]{1,0:T(8,128)(2,1)S(1)} %get-tuple-element.60), channel_id=1, source_target_pairs={{8,0},{10,2},{9,1},{11,3},{12,4},{14,6},{13,5},{15,7},{0,8},{2,10}... | collective-permute-start | bytes 294920 | tf_op jit(solution)/shard_map/ppermute | solution.py:48
  89.2 6.2 %collective-permute-start.24 = (bf16[32,1536]{1,0:T(8,128)(2,1)S(1)}, bf16[32,1536]{1,0:T(8,128)(2,1)S(1)}, u32[]{:S(2)}, u32[]{:S(2)}) collective-permute-start(bf16[32,1536]{1,0:T(8,128)(2,1)S(1)} %get-tuple-element.61), channel_id=1, source_target_pairs={{4,0},{6,2},{5,1},{7,3},{8,4},{10,6},{9,5},{11,7},{12,8},{14,10},{... | collective-permute-start | bytes 294920 | tf_op jit(solution)/shard_map/ppermute | solution.py:48
  91.3 5.8 %collective-permute-start.25 = (bf16[32,1536]{1,0:T(8,128)(2,1)S(1)}, bf16[32,1536]{1,0:T(8,128)(2,1)S(1)}, u32[]{:S(2)}, u32[]{:S(2)}) collective-permute-start(bf16[32,1536]{1,0:T(8,128)(2,1)S(1)} %get-tuple-element.62), channel_id=1, source_target_pairs={{12,0},{14,2},{13,1},{15,3},{0,4},{2,6},{1,5},{3,7},{4,8},{6,10},{... | collective-permute-start | bytes 294920 | tf_op jit(solution)/shard_map/ppermute | solution.py:48
  (14 other events, 79.8 us)
